TPU v7x, 256 devices: a whole 4x4x8 slice. The times are simulated.
256 devices in a mesh: grp: 16 (over x, y_hi, core), shard: 16 (over z, y_lo).
Axes of the slice: x: 4, y: 4 (y_hi: 2, y_lo: 2; y = y_hi * 2 + y_lo), z: 8, core: 2. Of those that a mesh axis runs over, the one named last changes fastest.
Arguments:
- entities: float32 [262144, 256], P(('grp', 'shard')), may hold values from -1.5 to 1.5
- row_acc: float32 [262144], P(('grp', 'shard')), may hold values from 0.01 to 0.1
- relations: float32 [4096, 256], replicated, may hold values from 0.1 to 1.9
- rel_acc: float32 [4096], replicated, may hold values from 0.0005 to 0.01
- src_row: int32 [2, 16, 16, 1152], P(None, 'grp', 'shard'), may hold values from 0 to 1023
- rel_id: int32 [2, 16, 16, 1152], P(None, 'grp', 'shard'), may hold values from 0 to 4095
- dst_owner: int32 [2, 16, 16, 1152, 1], P(None, 'grp', 'shard'), may hold values from 0 to 15; in each aligned block of 1152 rows (0 to 1151, 1152 to 2303, ..., all dimensions but the last counted through in order) at most 144 rows name the same one
- dst_row: int32 [2, 16, 16, 1152], P(None, 'grp', 'shard'), may hold values from 0 to 1023
- neg_rows: int32 [2, 16, 1024], P(None, 'grp', 'shard'), may hold values from 0 to 1023
- lengths: int32 [2, 16, 16], P(None, 'grp', 'shard'), may hold values from 1 to 1152, 6144 in all within a row
Outputs:
- new_entities: float32 [262144, 256], P(('grp', 'shard'))
- new_row_acc: float32 [262144], P(('grp', 'shard'))
- new_relations: float32 [4096, 256], replicated
- new_rel_acc: float32 [4096], replicated
Inputs may be any that keep to these rules, and one draw needn't show every extreme that they name: `dst_owner`: at most 144 of one device's 1152 edge slots name one shard index; some device reaches it. In each round a group's 16 lengths sum to 6144 and the largest is 1152; a device's live edges are its first slots. `src_row`: the edge slots of device (g, s) have sources among that device's own rows.
All inputs are finite; a program needn't handle non-finite values.
Results may differ from a plain program's by a relative error of at most 0.0045.
Values may be sent and summed in bfloat16 or wider, within the bound.
A program may use at most 128 MiB of HBM per device.

v0:
```python
import jax
import jax.numpy as jnp
from jax import lax
from jax.sharding import PartitionSpec as P

LEARN_RATE = 0.3


def passed_along(block, axis, distance):
    devices = range(lax.axis_size(axis))
    route = [((i - distance) % len(devices), i) for i in devices]
    return lax.ppermute(block, axis, route)


def adagrad(table, accum, gradient):
    total = accum + jnp.mean(gradient * gradient, axis=-1)
    return (table - LEARN_RATE * gradient / jnp.sqrt(total)[..., None], total)


def score_edges(src_emb, dst_emb, rel_rows, live_mask, negatives):
    query = src_emb.astype(jnp.float32) * rel_rows
    query_bf = query.astype(jnp.bfloat16)
    positive = jnp.sum(query * dst_emb.astype(jnp.float32), axis=-1)
    negative_sc = lax.dot_general(
        query_bf, negatives, (((1,), (1,)), ((), ())), preferred_element_type=jnp.float32
    )
    pos_weight = jnp.where(live_mask, -jax.nn.sigmoid(-positive), 0.0)
    neg_weight = jnp.where(
        live_mask[:, None], jax.nn.sigmoid(negative_sc) / negatives.shape[0], 0.0
    ).astype(jnp.bfloat16)
    query_grad = pos_weight[:, None] * dst_emb.astype(jnp.float32) + jnp.dot(
        neg_weight, negatives, preferred_element_type=jnp.float32
    )
    return (
        query_grad * rel_rows,
        query_grad * src_emb.astype(jnp.float32),
        pos_weight[:, None] * query,
        query_bf,
        neg_weight,
    )


def bucket(
    src_table, dst_table, relations, src_row, rel_id, dst_owner, dst_row, neg_rows, lengths, turn
):
    src_rows = src_row[turn, 0, 0]
    rel_ids = rel_id[turn, 0, 0]
    owners = dst_owner[turn, 0, 0, :, 0]
    dst_rows = dst_row[turn, 0, 0]
    neg_local = neg_rows[turn, 0]
    live_len = lengths[turn, 0, 0]
    shards = lax.axis_size("shard")
    edges = src_rows.shape[0]
    width = src_table.shape[1]
    capacity = 2 * edges // shards
    positions = jnp.arange(edges, dtype=jnp.int32)
    live_mask = positions < live_len
    src_emb = jnp.take(src_table, src_rows, axis=0).astype(jnp.bfloat16)
    chosen = (owners[:, None] == jnp.arange(shards, dtype=jnp.int32)[None, :]).astype(jnp.int32)
    ranks = jnp.sum((jnp.cumsum(chosen, axis=0) - 1) * chosen, axis=1)
    request = jnp.zeros((shards, capacity), jnp.int32).at[owners, ranks].set(dst_rows)
    asked = lax.all_to_all(request, "shard", split_axis=0, concat_axis=0, tiled=True)
    looked = jnp.take(dst_table, asked, axis=0)
    fetched, asked = (
        lax.all_to_all(looked, "shard", split_axis=0, concat_axis=0, tiled=True),
        asked,
    )
    dst_emb = fetched[owners, ranks]
    own_negs = jnp.take(dst_table, neg_local, axis=0)
    negatives = lax.all_gather(own_negs, "shard", axis=0, tiled=True)
    rel_rows = jnp.take(relations, rel_ids, axis=0)
    src_grad, rel_grad_rows, dst_grad, query_bf, neg_weight = score_edges(
        src_emb, dst_emb, rel_rows, live_mask, negatives
    )
    rel_grad = jax.ops.segment_sum(rel_grad_rows, rel_ids, num_segments=relations.shape[0])
    neg_grad = lax.psum_scatter(
        lax.dot_general(
            neg_weight, query_bf, (((0,), (0,)), ((), ())), preferred_element_type=jnp.float32
        ).astype(jnp.bfloat16),
        "shard",
        scatter_dimension=0,
        tiled=True,
    ).astype(jnp.float32)
    outgoing = jnp.zeros((shards, capacity, width), jnp.float32).at[owners, ranks].set(dst_grad)
    incoming = lax.all_to_all(outgoing, "shard", split_axis=0, concat_axis=0, tiled=True)
    zero_rows = jnp.zeros(src_table.shape, jnp.float32)
    dst_total = (
        zero_rows.at[asked.reshape(-1)].add(incoming.reshape(-1, width)).at[neg_local].add(neg_grad)
    )
    src_total = zero_rows.at[src_rows].add(src_grad)
    return (src_total, dst_total, rel_grad)


def sum_relations(gradient):
    return lax.psum(gradient, ("grp", "shard"))


def per_device(
    entities, row_acc, relations, rel_acc, src_row, rel_id, dst_owner, dst_row, neg_rows, lengths
):
    first_src, first_dst, first_rel = bucket(
        entities,
        entities.astype(jnp.bfloat16),
        relations,
        src_row,
        rel_id,
        dst_owner,
        dst_row,
        neg_rows,
        lengths,
        0,
    )
    table_one, accum_one = adagrad(entities, row_acc, first_src + first_dst)
    partner = passed_along(table_one.astype(jnp.bfloat16), "grp", -1)
    second_src, second_dst, second_rel = bucket(
        table_one, partner, relations, src_row, rel_id, dst_owner, dst_row, neg_rows, lengths, 1
    )
    carried = passed_along(second_dst, "grp", 1)
    table_two, accum_two = adagrad(table_one, accum_one, second_src + carried)
    rel_total = sum_relations(first_rel) + sum_relations(second_rel)
    new_rel, new_racc = adagrad(relations, rel_acc, rel_total)
    return (table_two, accum_two, new_rel, new_racc)


def solution(mesh):
    in_specs = (
        P(("grp", "shard"), None),
        P(("grp", "shard")),
        P(),
        P(),
        P(None, "grp", "shard", None),
        P(None, "grp", "shard", None),
        P(None, "grp", "shard", None, None),
        P(None, "grp", "shard", None),
        P(None, "grp", "shard"),
        P(None, "grp", "shard"),
    )
    out_specs = (P(("grp", "shard"), None), P(("grp", "shard")), P(), P())
    return jax.shard_map(
        per_device, mesh=mesh, in_specs=in_specs, out_specs=out_specs, check_vma=False
    )
```

profile of v0, /device:TPU:1, one launch (start us, length us, event | category | flops | bytes accessed | tf_op | source)
XLA Modules:
  0.0 875.5 jit_solution(1522524260634359922)
XLA Ops:
  26.2 10.1 %all-to-all-start = ((s32[16,1,144]{2,1,0:T(1,128)}), s32[16,1,144]{2,1,0:T(1,128)S(1)}, u32[]{:S(2)}, u32[]{:S(2)}) async-start(s32[16,1,144]{2,1,0:T(1,128)} %all_to_all.28), calls=%async_computation | async-start | bytes 32768 | tf_op jit(solution)/shard_map/all_to_all | solution.py:62
  36.4 7.3 all-to-all-done
  43.9 6.9 gather_fusion.4
  67.2 16.4 %all-to-all-done.1 = bf16[16,144,256]{2,1,0:T(8,128)(2,1)} async-done(((bf16[16,144,256]{2,1,0:T(8,128)(2,1)}), bf16[16,144,256]{2,1,0:T(8,128)(2,1)}, u32[]{:S(2)}, u32[]{:S(2)}) %all-to-all-start.1) | async-done | bytes 1179680 | tf_op jit(solution)/shard_map/all_to_all | solution.py:65
  83.7 16.4 %gather_fusion = bf16[1152,256]{1,0:T(8,128)(2,1)S(1)} fusion(bf16[16,144,256]{2,1,0:T(8,128)(2,1)} %all-to-all-done.1, s32[1152]{0:T(1024)S(1)} %get-tuple-element.11), kind=kCustom, calls=%fused_computation.8 | custom fusion | bytes 1188864 | tf_op jit(solution)/shard_map/gather | solution.py:68
  103.4 13.4 %scatter_custom_fusion.9 = f32[2304,256]{1,0:T(8,128)} fusion(s32[1152]{0:T(1024)S(1)} %broadcast_select_fusion.5, f32[]{:T(128)} %constant.24.clone.1, f32[1152,256]{1,0:T(8,128)} %get-tuple-element.35, f32[1152]{0:T(1024)S(1)} %negate_select_fusion.1), kind=kCustom, calls=%fused_computation.48 | custom fusion | flops 294912 | bytes 3547140
  116.9 7.5 all-to-all-start.2
  125.9 75.3 %all_gather.6 = bf16[1024,256]{1,0:T(8,128)(2,1)S(1)} all-gather(bf16[64,256]{1,0:T(8,128)(2,1)S(1)} %broadcast_select_fusion.3), channel_id=1, replica_groups=mesh['grp'=16,'shard'=16] {'shard'}, dimensions={0}, use_global_device_ids=true | all-gather | bytes 557056 | tf_op jit(solution)/shard_map/all_gather | solution.py:70
  217.2 11.1 %scatter_custom_fusion = f32[1024,256]{1,0:T(8,128)S(1)} fusion(s32[1152]{0:T(1024)S(1)} %get-tuple-element.9, f32[1152,256]{1,0:T(8,128)} %convolution_add_fusion.1, f32[1152,256]{1,0:T(8,128)S(1)} %copy-done.2, f32[]{:T(128)} %constant.15.clone.2, pred[1152]{0:T(1024)(128)(4,1)S(1)} %get-tuple-element.52, f32[]{:T(128)} %constant.24.clone.1), kind=kCustom, calls=%fused_computation.54 | custom fusion | flops 884736 | bytes 3409928 | tf_op jit(solution)/shard_map/scatter-add | solution.py:90
  235.2 15.8 %scatter_custom_fusion.1 = f32[1024,256]{1,0:T(8,128)S(1)} fusion(s32[2304]{0:T(1024)S(1)} %fusion.43, f32[2304,256]{1,0:T(8,128)} %bitcast.7, f32[]{:T(128)} %constant.24.clone.1), kind=kCustom, calls=%fused_computation.72 | custom fusion | flops 589824 | bytes 1049088 | tf_op jit(solution)/shard_map/scatter-add | solution.py:88
  250.9 21.4 %reduce-scatter.3.cloned.1.call-done = bf16[64,256]{1,0:T(8,128)(2,1)} async-done(((bf16[1024,256]{1,0:T(8,128)(2,1)}), bf16[64,256]{1,0:T(8,128)(2,1)}) %reduce-scatter.3.cloned.1.call-update) | async-done | bytes 32784 | tf_op jit(solution)/shard_map/reduce_scatter | solution.py:76
  277.2 20.4 %collective-permute-start = (bf16[1024,256]{1,0:T(8,128)(2,1)}, bf16[1024,256]{1,0:T(8,128)(2,1)S(1)}, u32[]{:S(2)}, u32[]{:S(2)}) collective-permute-start(bf16[1024,256]{1,0:T(8,128)(2,1)} %get-tuple-element.32), channel_id=1, source_target_pairs={{16,0},{32,16},{48,32},{64,48},{80,64},{96,80},{112,96},{128,112},... | collective-permute-start | bytes 1572872 | tf_op jit(solution)/shard_map/ppermute | solution.py:12
  297.7 9.2 %collective-permute-done = bf16[1024,256]{1,0:T(8,128)(2,1)S(1)} collective-permute-done((bf16[1024,256]{1,0:T(8,128)(2,1)}, bf16[1024,256]{1,0:T(8,128)(2,1)S(1)}, u32[]{:S(2)}, u32[]{:S(2)}) %collective-permute-start) | collective-permute-done | bytes 524320 | tf_op jit(solution)/shard_map/ppermute | solution.py:12
  325.7 14.3 %scatter_custom_fusion.6 = f32[4096,256]{1,0:T(8,128)} fusion(s32[1152]{0:T(1024)S(1)} %get-tuple-element.15, f32[]{:T(128)} %constant.24.clone.1, f32[1152,256]{1,0:T(8,128)} %convolution_add_fusion.1, f32[1152,256]{1,0:T(8,128)} %copy-done.1, pred[1152]{0:T(1024)(128)(4,1)S(1)} %get-tuple-element.53), kind=kCustom, calls=%fused_computation.30 | custom fusion | flops 1179648 | bytes 6555652 | tf_op jit(solution)/shard_map/scatter-add | solution.py:75
  349.6 16.3 %gather_fusion.1 = bf16[1152,256]{1,0:T(8,128)(2,1)S(1)} fusion(bf16[16,144,256]{2,1,0:T(8,128)(2,1)} %all-to-all-done.4, s32[1152]{0:T(1024)S(1)} %get-tuple-element.10), kind=kCustom, calls=%fused_computation.9 | custom fusion | bytes 1188864 | tf_op jit(solution)/shard_map/gather | solution.py:68
  369.4 13.5 %scatter_custom_fusion.11 = f32[2304,256]{1,0:T(8,128)} fusion(s32[1152]{0:T(1024)S(1)} %broadcast_select_fusion.4, f32[]{:T(128)} %constant.24.clone.1, f32[1152,256]{1,0:T(8,128)} %get-tuple-element.31, f32[1152]{0:T(1024)S(1)} %negate_select_fusion), kind=kCustom, calls=%fused_computation.46 | custom fusion | flops 294912 | bytes 3547140
  387.4 77.5 %all_gather.7 = bf16[1024,256]{1,0:T(8,128)(2,1)S(1)} all-gather(bf16[64,256]{1,0:T(8,128)(2,1)S(1)} %broadcast_select_fusion.2), channel_id=1, replica_groups=mesh['grp'=16,'shard'=16] {'shard'}, dimensions={0}, use_global_device_ids=true | all-gather | bytes 557056 | tf_op jit(solution)/shard_map/all_gather | solution.py:70
  470.9 14.2 %scatter_custom_fusion.7 = f32[4096,256]{1,0:T(8,128)} fusion(s32[1152]{0:T(1024)S(1)} %get-tuple-element.14, f32[]{:T(128)} %constant.24.clone.1, f32[1152,256]{1,0:T(8,128)} %convolution_add_fusion, f32[1152,256]{1,0:T(8,128)} %gather_fusion.6, pred[1152]{0:T(1024)(128)(4,1)S(1)} %compare_and_fusion.3), kind=kCustom, calls=%fused_computation.28 | custom fusion | flops 1179648 | bytes 6555652 | tf_op jit(solution)/shard_map/scatter-add | solution.py:75
  495.1 268.4 %all-reduce.2.cloned.1.call-done = f32[4096,256]{1,0:T(8,128)} async-done(((f32[4096,256]{1,0:T(8,128)}), f32[4096,256]{1,0:T(8,128)}) %all-reduce.2.cloned.1.call-update) | async-done | bytes 4194320 | tf_op jit(solution)/shard_map/psum | solution.py:95
  766.9 16.6 %scatter_custom_fusion.3 = f32[1024,256]{1,0:T(8,128)} fusion(s32[2304]{0:T(1024)S(1)} %fusion.44, f32[2304,256]{1,0:T(8,128)} %bitcast.15, f32[]{:T(128)} %constant.24.clone.1), kind=kCustom, calls=%fused_computation.70 | custom fusion | flops 589824 | bytes 1049088 | tf_op jit(solution)/shard_map/scatter-add | solution.py:88
  783.6 41.6 %reduce-scatter.5.cloned.1.call-done = bf16[64,256]{1,0:T(8,128)(2,1)} async-done(((bf16[1024,256]{1,0:T(8,128)(2,1)}), bf16[64,256]{1,0:T(8,128)(2,1)}) %reduce-scatter.5.cloned.1.call-update) | async-done | bytes 32784 | tf_op jit(solution)/shard_map/reduce_scatter | solution.py:76
  828.4 14.7 %collective-permute-start.1 = (f32[1024,256]{1,0:T(8,128)}, f32[1024,256]{1,0:T(8,128)S(1)}, u32[]{:S(2)}, u32[]{:S(2)}) collective-permute-start(f32[1024,256]{1,0:T(8,128)} %scatter_custom_fusion.4), channel_id=1, source_target_pairs={{240,0},{0,16},{16,32},{32,48},{48,64},{64,80},{80,96},{96,112},{1... | collective-permute-start | bytes 3145736 | tf_op jit(solution)/shard_map/ppermute | solution.py:12
  848.3 6.9 collective-permute-done.1
  855.2 11.3 %scatter_custom_fusion.5 = f32[1024,256]{1,0:T(8,128)S(1)} fusion(f32[1024,256]{1,0:T(8,128)S(1)} %collective-permute-done.1, s32[1152]{0:T(1024)S(1)} %get-tuple-element.8, f32[1152,256]{1,0:T(8,128)} %convolution_add_fusion, f32[1152,256]{1,0:T(8,128)S(1)} %gather_fusion.7, f32[]{:T(128)} %constant.15.clone.2, pred[1152]{0:T(1024)(128)(4,1)S(1)} %compare_and_fusion.2), kind=kCustom, calls=%fused_computation.50 | custom fusion | flops 884736 | bytes 3409924 | tf_op jit(solution)/shard_map/scatter-add | solution.py:90
  (140 shorter events, 133.8 us)
Async XLA Ops:
  7.2 11.6 %copy-start.15 = (s32[2]{0:T(128)S(1)}, s32[2]{0:T(128)}, u32[]{:S(2)}) copy-start(s32[2]{0:T(128)} %constant.94) | copy-start | bytes 28
  7.2 11.7 %copy-start.14 = (s32[2]{0:T(128)S(1)}, s32[2]{0:T(128)}, u32[]{:S(2)}) copy-start(s32[2]{0:T(128)} %constant.63) | copy-start | bytes 28
  7.2 11.5 %copy-start.7 = (s32[2,1,1,1152,1]{3,4,2,1,0:T(1,128)S(1)}, s32[2,1,1,1152,1]{3,4,2,1,0:T(1,128)}, u32[]{:S(2)}) copy-start(s32[2,1,1,1152,1]{3,4,2,1,0:T(1,128)} %param.24) | copy-start | bytes 27652
  7.2 11.8 %copy-start.10 = (s32[2,1,1,1152]{3,2,1,0:T(1,128)S(1)}, s32[2,1,1,1152]{3,2,1,0:T(1,128)}, u32[]{:S(2)}) copy-start(s32[2,1,1,1152]{3,2,1,0:T(1,128)} %param.25) | copy-start | bytes 27652
  7.2 29.1 %copy-start = (f32[1024,256]{1,0:T(8,128)S(1)}, f32[1024,256]{1,0:T(8,128)}, u32[]{:S(2)}) copy-start(f32[1024,256]{1,0:T(8,128)} %param.18) | copy-start | bytes 3145732
  26.2 17.5 %all-to-all-start = ((s32[16,1,144]{2,1,0:T(1,128)}), s32[16,1,144]{2,1,0:T(1,128)S(1)}, u32[]{:S(2)}, u32[]{:S(2)}) async-start(s32[16,1,144]{2,1,0:T(1,128)} %all_to_all.28), calls=%async_computation | async-start | bytes 32768 | tf_op jit(solution)/shard_map/all_to_all | solution.py:62
  52.0 4.5 copy-start.6
  52.0 31.6 %all-to-all-start.1 = ((bf16[16,144,256]{2,1,0:T(8,128)(2,1)}), bf16[16,144,256]{2,1,0:T(8,128)(2,1)}, u32[]{:S(2)}, u32[]{:S(2)}) async-start(bf16[16,144,256]{2,1,0:T(8,128)(2,1)} %broadcast_select_fusion.1), calls=%async_computation.1 | async-start | bytes 2359296 | tf_op jit(solution)/shard_map/all_to_all | solution.py:65
  56.6 3.3 copy-start.11
  59.9 40.1 %copy-start.1 = (f32[1152,256]{1,0:T(8,128)}, f32[1152,256]{1,0:T(8,128)S(1)}, u32[]{:S(2)}) copy-start(f32[1152,256]{1,0:T(8,128)S(1)} %gather_fusion.2) | copy-start | bytes 3538948
  60.0 6.6 copy-start.13
  116.9 7.5 copy-start.12
  116.9 84.3 %copy-start.4 = (f32[1152,256]{1,0:T(8,128)S(1)}, f32[1152,256]{1,0:T(8,128)}, u32[]{:S(2)}) copy-start(f32[1152,256]{1,0:T(8,128)} %get-tuple-element.35) | copy-start | bytes 3538948
  116.9 111.5 %all-to-all-start.2 = ((f32[16,144,256]{2,1,0:T(8,128)}), f32[16,144,256]{2,1,0:T(8,128)}, u32[]{:S(2)}, u32[]{:S(2)}) async-start(f32[16,144,256]{2,1,0:T(8,128)} %bitcast.80), calls=%async_computation.2 | async-start | bytes 4718592 | tf_op jit(solution)/shard_map/all_to_all | solution.py:85
  124.3 148.0 %reduce-scatter.3.cloned.1.call-start = ((), (), s32[]{:S(2)}) async-start(), calls=%async_computation.8 | async-start | bytes 557056 | tf_op jit(solution)/shard_map/reduce_scatter | solution.py:76
  213.6 3.7 copy-start.2
  228.4 69.2 %all-to-all-start.3 = ((s32[16,1,144]{2,1,0:T(1,128)}), s32[16,1,144]{2,1,0:T(1,128)S(1)}, u32[]{:S(2)}, u32[]{:S(2)}) async-start(s32[16,1,144]{2,1,0:T(1,128)} %all_to_all.33), calls=%async_computation.4 | async-start | bytes 32768 | tf_op jit(solution)/shard_map/all_to_all | solution.py:62
  277.2 29.8 %collective-permute-start = (bf16[1024,256]{1,0:T(8,128)(2,1)}, bf16[1024,256]{1,0:T(8,128)(2,1)S(1)}, u32[]{:S(2)}, u32[]{:S(2)}) collective-permute-start(bf16[1024,256]{1,0:T(8,128)(2,1)} %get-tuple-element.32), channel_id=1, source_target_pairs={{16,0},{32,16},{48,32},{64,48},{80,64},{96,80},{112,96},{128,112},... | collective-permute-start | bytes 1572872 | tf_op jit(solution)/shard_map/ppermute | solution.py:12
  315.1 34.5 %all-to-all-start.4 = ((bf16[16,144,256]{2,1,0:T(8,128)(2,1)}), bf16[16,144,256]{2,1,0:T(8,128)(2,1)}, u32[]{:S(2)}, u32[]{:S(2)}) async-start(bf16[16,144,256]{2,1,0:T(8,128)(2,1)} %broadcast_select_fusion), calls=%async_computation.5 | async-start | bytes 2359296 | tf_op jit(solution)/shard_map/all_to_all | solution.py:65
  382.9 384.0 %all-to-all-start.5 = ((f32[16,144,256]{2,1,0:T(8,128)}), f32[16,144,256]{2,1,0:T(8,128)}, u32[]{:S(2)}, u32[]{:S(2)}) async-start(f32[16,144,256]{2,1,0:T(8,128)} %bitcast.81), calls=%async_computation.6 | async-start | bytes 4718592 | tf_op jit(solution)/shard_map/all_to_all | solution.py:85
  387.4 376.1 %all-reduce.2.cloned.1.call-start = ((), (), s32[]{:S(2)}) async-start(), calls=%async_computation.10 | async-start | bytes 8388608 | tf_op jit(solution)/shard_map/psum | solution.py:95
  491.2 334.0 %reduce-scatter.5.cloned.1.call-start = ((), (), s32[]{:S(2)}) async-start(), calls=%async_computation.9 | async-start | bytes 557056 | tf_op jit(solution)/shard_map/reduce_scatter | solution.py:76
  495.1 271.2 %copy-start.9 = (f32[4096]{0:T(1024)S(1)}, f32[4096]{0:T(1024)}, u32[]{:S(2)}) copy-start(f32[4096]{0:T(1024)} %param.21) | copy-start | bytes 49156
  828.4 26.8 %collective-permute-start.1 = (f32[1024,256]{1,0:T(8,128)}, f32[1024,256]{1,0:T(8,128)S(1)}, u32[]{:S(2)}, u32[]{:S(2)}) collective-permute-start(f32[1024,256]{1,0:T(8,128)} %scatter_custom_fusion.4), channel_id=1, source_target_pairs={{240,0},{0,16},{16,32},{32,48},{48,64},{64,80},{80,96},{96,112},{1... | collective-permute-start | bytes 3145736 | tf_op jit(solution)/shard_map/ppermute | solution.py:12
  (5 other events, 6.5 us)
Sparse Core Ops, SparseCore 0:
  206.3 65.9 reduce-scatter.2
  491.3 272.1 all-reduce.1
  766.0 59.0 reduce-scatter.4
where the time goes:
time: 886 us; the launch traced here: 875 us
  waiting for transfers between devices  376 us (42%)
  other arithmetic  155 us (17%)
  blocking collectives  153 us (17%)
  local copies, waits for them, and re-layouts  87.9 us (10%)
  starting transfers between devices  73 us (8%)
  matrix products  15.4 us (2%)
  between operations  14.9 us (2%)
    psum x1, waiting for transfers between devices, sum_relations(): return lax.psum(gradient, ('grp', 'shard'))  268 us
    all_gather x2, blocking collectives, bucket(): negatives = lax.all_gather(own_negs, 'shard', axis=0, tiled=True)  153 us
    reduce_scatter x2, waiting for transfers between devices, bucket(): lax.psum_scatter(lax.dot_general(neg_weight, query_bf, (((0,), (0,)), (()...  62.9 us
    scatter-add x4, other arithmetic, bucket(): zero_rows.at[asked.reshape(-1)].add(incoming.reshape(-1, width))  37.3 us
    ppermute x2, starting transfers between devices, passed_along(): return lax.ppermute(block, axis, route)  35.2 us
    gather x2, local copies, waits for them, and re-layouts, bucket(): dst_emb = fetched[owners, ranks]  32.7 us
    scatter-add x2, other arithmetic, bucket(): jax.ops.segment_sum(rel_grad_rows, rel_ids, num_segments=relations.shape[0])  28.6 us
    unnamed x6, other arithmetic  27.2 us
  transfers between devices with their start and end apart: 11, of which 8 were waited for; matrix products, arithmetic and copies ran while one was open for 16% of the time, Pallas kernels for 0%

commit v1 on v0

v1 whole, which is shorter than its diff:
```python
import functools
import jax
import jax.numpy as jnp
from jax import lax
from jax.experimental import pallas as pl
from jax.experimental.pallas import tpu as pltpu
from jax.sharding import PartitionSpec as P

LEARN_RATE = 0.3
MESH = pl.DeviceIdType.MESH
F32 = jnp.float32
BF16 = jnp.bfloat16
LANES = 256


def adagrad(table, accum, gradient):
    total = accum + jnp.mean(gradient * gradient, axis=-1)
    return (table - LEARN_RATE * gradient / jnp.sqrt(total)[..., None], total)


def dot(a, b):
    return jnp.dot(a, b, preferred_element_type=F32)


def hot(index, size):
    places = lax.broadcasted_iota(jnp.int32, (index.shape[0], size), 1)
    return jnp.where(places == index, 1.0, 0.0).astype(BF16)


def hot_t(index, size, first=0):
    places = lax.broadcasted_iota(jnp.int32, (size, index.shape[1]), 0) + first
    return jnp.where(places == index, 1.0, 0.0).astype(BF16)


def bucket_kernel(turn, groups, shards, edges, capacity, *refs):
    refs = list(refs)
    take = lambda n: [refs.pop(0) for _ in range(n)]
    table, relations, meta, requests = take(4)
    rel_prev = take(1)[0] if turn else None
    total_out, rel_out = take(2)
    asked_next = None if turn else take(1)[0]
    (asked, meta_t, own_negs, negs, sent, got, back, neg_send, neg_got, src_emb, rel_rows,
     query_bf, query_grad, src_grad, rel_grad, dst_grad, neg_acc, high, low) = take(19)
    if turn:
        half, rel_got_c, got_x, got_y, sum_x, sum_y, got_x2, got_y2, last, got_z = take(10)
    (req_send, req_recv, neg_send_sem, neg_recv_sem, row_send, row_recv, ngr_send, ngr_recv,
     grad_send, grad_recv, next_sem) = take(11)
    if turn:
        rel_send, rel_recv = take(2)

    rows, width = table.shape
    n_rel = relations.shape[0]
    n_own = own_negs.shape[0]
    n_neg = negs.shape[0]
    g, s = lax.axis_index("grp"), lax.axis_index("shard")
    next_g, prev_g = lax.rem(g + 1, groups), lax.rem(g + groups - 1, groups)
    to_g = prev_g if turn else g
    from_g = next_g if turn else g
    first = 0 if turn else 1
    tile = edges // 3
    chunk = lambda ref, i, size: ref.at[pl.ds(pl.multiple_of(i * size, 16), size)]

    x, y_hi, core = g // 4, lax.rem(g // 2, 2), lax.rem(g, 2)
    z, y_lo = s // 2, lax.rem(s, 2)
    y = y_hi * 2 + y_lo

    def device(x, y, z, core):
        return (x * 4 + (y // 2) * 2 + core, z * 2 + lax.rem(y, 2))

    x_at = lambda k: lax.rem(x + k, 4)
    y_at = lambda k: lax.rem(y + k, 4)
    z_at = lambda k: lax.rem(z + k, 8)
    x_dev = lambda k: device(x_at(k), y, z, core)
    y_dev = lambda k: device(x, y_at(k), z, core)
    z_dev = lambda k: device(x, y, z_at(k), core)
    core_dev = device(x, y, z, 1 - core)

    barrier = pltpu.get_barrier_semaphore()

    def greet(k, carry):
        source = lax.rem(s + shards - k, shards)
        pl.semaphore_signal(barrier, inc=1, device_id=(from_g, source), device_id_type=MESH)
        return carry

    lax.fori_loop(first, shards, greet, 0)
    greeted = shards - first
    if turn:
        others = [core_dev] + [x_dev(k) for k in (1, 2, 3)] + [y_dev(k) for k in (1, 2, 3)]
        others += [z_dev(k) for k in range(1, 8)]
    else:
        others = [(prev_g, s)]
    for other in others:
        pl.semaphore_signal(barrier, inc=1, device_id=other, device_id_type=MESH)
    greeted += len(others)

    meta_t[...] = jnp.transpose(meta[...])
    neg_col = jnp.transpose(requests[shards])[:n_own, turn : turn + 1]
    own_negs[...] = dot(hot(neg_col, rows), table[...]).astype(BF16)
    pl.semaphore_wait(barrier, greeted)

    def request_copy(k):
        target = lax.rem(s + k, shards)
        return pltpu.make_async_remote_copy(
            src_ref=requests.at[target], dst_ref=asked.at[s],
            send_sem=req_send.at[k], recv_sem=req_recv.at[k],
            device_id=(g, target), device_id_type=MESH,
        )

    def neg_copy(k):
        return pltpu.make_async_remote_copy(
            src_ref=own_negs, dst_ref=chunk(negs, s, n_own),
            send_sem=neg_send_sem.at[k], recv_sem=neg_recv_sem.at[k],
            device_id=(to_g, lax.rem(s + k, shards)), device_id_type=MESH,
        )

    def row_copy(k):
        target = lax.rem(s + k, shards)
        return pltpu.make_async_remote_copy(
            src_ref=chunk(sent, target, capacity), dst_ref=chunk(got, s, capacity),
            send_sem=row_send.at[k], recv_sem=row_recv.at[k],
            device_id=(to_g, target), device_id_type=MESH,
        )

    def neg_grad_copy(k):
        target = lax.rem(s + k, shards)
        return pltpu.make_async_remote_copy(
            src_ref=chunk(neg_send, target, n_own), dst_ref=chunk(neg_got, s, n_own),
            send_sem=ngr_send.at[k], recv_sem=ngr_recv.at[k],
            device_id=(from_g, target), device_id_type=MESH,
        )

    def grad_copy(k):
        target = lax.rem(s + k, shards)
        return pltpu.make_async_remote_copy(
            src_ref=chunk(sent, target, capacity), dst_ref=chunk(back, s, capacity),
            send_sem=grad_send.at[k], recv_sem=grad_recv.at[k],
            device_id=(from_g, target), device_id_type=MESH,
        )

    def each(begin, body):
        def step(k, carry):
            body(k)
            return carry

        lax.fori_loop(begin, shards, step, 0)

    if turn == 0:
        each(1, lambda k: request_copy(k).start())
        asked[s] = requests[s]
        asked[shards] = requests[shards]
        negs[pl.ds(pl.multiple_of(s * n_own, 16), n_own), :] = own_negs[...]
    else:
        asked[...] = requests[...]
    each(first, lambda k: neg_copy(k).start())

    if turn == 0:
        each(1, lambda k: request_copy(k).wait())
        forward = pltpu.make_async_remote_copy(
            src_ref=asked, dst_ref=asked_next, send_sem=next_sem.at[0], recv_sem=next_sem.at[1],
            device_id=(next_g, s), device_id_type=MESH,
        )
        forward.start()

    def answer(who):
        column = jnp.transpose(asked[who])[:capacity, turn : turn + 1]
        return dot(hot(column, rows), table[...]).astype(BF16)

    def send_rows(k):
        target = lax.rem(s + k, shards)
        sent[pl.ds(pl.multiple_of(target * capacity, 16), capacity), :] = answer(target)
        row_copy(k).start()

    each(first, send_rows)
    if turn == 0:
        got[pl.ds(pl.multiple_of(s * capacity, 16), capacity), :] = answer(s)

    def split(i, carry):
        at = pl.ds(i * 512, 512)
        value = relations[at, :]
        upper = value.astype(BF16)
        high[at, :] = upper
        low[at, :] = (value - upper.astype(F32)).astype(BF16)
        return carry

    lax.fori_loop(0, n_rel // 512, split, 0)

    def look(i, carry):
        at = pl.ds(pl.multiple_of(i * tile, 128), tile)
        columns = meta_t[at, :]
        emb = dot(hot(columns[:, 1:2], rows), table[...])
        picked = hot(columns[:, 3:4], n_rel)
        rel = dot(picked, high[...]) + dot(picked, low[...])
        src_emb[at, :] = emb.astype(BF16)
        rel_rows[at, :] = rel
        query_bf[at, :] = (emb * rel).astype(BF16)
        return carry

    lax.fori_loop(0, 3, look, 0)

    each(first, lambda k: neg_copy(k).wait())
    neg_acc[...] = jnp.zeros_like(neg_acc)

    def against_negatives(i, carry):
        at = pl.ds(pl.multiple_of(i * tile, 128), tile)
        query = query_bf[at, :]
        scores = lax.dot_general(
            query, negs[...], (((1,), (1,)), ((), ())), preferred_element_type=F32
        )
        live = meta_t[at, :][:, 2:3] > 0
        weight = jnp.where(live, (jnp.tanh(scores * 0.5) + 1.0) * (0.5 / n_neg), 0.0).astype(BF16)
        query_grad[at, :] = dot(weight, negs[...])
        neg_acc[...] += dot(jnp.transpose(query.astype(F32)).astype(BF16), weight)
        return carry

    lax.fori_loop(0, 3, against_negatives, 0)
    neg_send[...] = jnp.transpose(neg_acc[...]).astype(BF16)
    if turn == 0:
        own = pl.ds(pl.multiple_of(s * n_own, 16), n_own)
        neg_got[own, :] = neg_send[own, :]
    each(first, lambda k: neg_grad_copy(k).start())
    each(first, lambda k: row_copy(k).wait_recv())

    def positives(i, carry):
        at = pl.ds(pl.multiple_of(i * tile, 128), tile)
        columns = meta_t[at, :]
        emb = src_emb[at, :].astype(F32)
        rel = rel_rows[at, :]
        query = emb * rel
        dst = dot(hot(columns[:, 0:1], shards * capacity), got[...])
        positive = jnp.sum(query * dst, axis=1, keepdims=True)
        weight = jnp.where(columns[:, 2:3] > 0, (jnp.tanh(positive * -0.5) + 1.0) * -0.5, 0.0)
        grad = weight * dst + query_grad[at, :]
        src_grad[at, :] = (grad * rel).astype(BF16)
        rel_grad[at, :] = (grad * emb).astype(BF16)
        dst_grad[at, :] = (weight * query).astype(BF16)
        return carry

    lax.fori_loop(0, 3, positives, 0)

    def scatter_relations(begin, count):
        def step(i, carry):
            at = pl.multiple_of(begin + i * 512, 512)
            part = dot(hot_t(meta[3:4, :], 512, at), rel_grad[...])
            if turn:
                part = part + rel_prev[pl.ds(at, 512), :].astype(F32)
                half[pl.ds(at, 512), :] = part.astype(BF16)
            else:
                rel_out[pl.ds(at, 512), :] = part.astype(BF16)
            return carry

        lax.fori_loop(0, count // 512, step, 0)

    def send_grads():
        each(first, lambda k: row_copy(k).wait_send())

        def block(target):
            return dot(hot_t(meta[0:1, :], capacity, target * capacity), dst_grad[...]).astype(BF16)

        def send(k):
            target = lax.rem(s + k, shards)
            sent[pl.ds(pl.multiple_of(target * capacity, 16), capacity), :] = block(target)
            grad_copy(k).start()

        each(first, send)
        if turn == 0:
            back[pl.ds(pl.multiple_of(s * capacity, 16), capacity), :] = block(s)

    def scatter_sources():
        def step(i, carry):
            at = pl.multiple_of(i * 256, 256)
            total_out[pl.ds(at, 256), :] = dot(hot_t(meta[1:2, :], 256, at), src_grad[...])
            return carry

        lax.fori_loop(0, rows // 256, step, 0)

    def take_grads():
        each(first, lambda k: neg_grad_copy(k).wait())
        summed = neg_got[0:n_own, :].astype(F32)
        for k in range(1, shards):
            summed += neg_got[k * n_own : (k + 1) * n_own, :].astype(F32)
        upper = summed.astype(BF16)
        lower = (summed - upper.astype(F32)).astype(BF16)
        picked = hot_t(asked[shards][turn : turn + 1, :n_own], rows)
        total_out[...] += dot(picked, upper) + dot(picked, lower)

        def add(who):
            picked = hot_t(asked[who][turn : turn + 1, :capacity], rows)
            block = back[pl.ds(pl.multiple_of(who * capacity, 16), capacity), :]
            total_out[...] += dot(picked, block)

        if turn == 0:
            add(s)

        def take_one(k):
            grad_copy(k).wait()
            add(lax.rem(s + shards - k, shards))

        each(first, take_one)

    if turn == 0:
        send_grads()
        scatter_sources()
        scatter_relations(0, n_rel)
        take_grads()
        forward.wait()
        return

    n_half, n_quarter = n_rel // 2, n_rel // 4
    big, small, least = n_quarter // 4, n_quarter // 16, n_rel // 256
    mine, theirs = core * n_half, (1 - core) * n_half

    def rel_copy(src, dst, sem, where):
        return pltpu.make_async_remote_copy(
            src_ref=src, dst_ref=dst, send_sem=rel_send.at[sem], recv_sem=rel_recv.at[sem],
            device_id=where, device_id_type=MESH,
        )

    span = lambda ref, at, size: ref.at[pl.ds(pl.multiple_of(at, 16), size)]

    def run(copies):
        for copy in copies:
            copy.start()
        return copies

    def finish(copies):
        for copy in copies:
            copy.wait()

    scatter_relations(theirs, n_half)
    copies = run([rel_copy(span(half, theirs, n_half), rel_got_c, 0, core_dev)])
    send_grads()
    scatter_relations(mine, n_half)
    finish(copies)

    def add_core(i, carry):
        at = pl.multiple_of(i * 256, 256)
        value = half[pl.ds(mine + at, 256), :].astype(F32) + rel_got_c[pl.ds(at, 256), :].astype(F32)
        rel_got_c[pl.ds(at, 256), :] = value.astype(BF16)
        return carry

    lax.fori_loop(0, n_half // 256, add_core, 0)
    chip = rel_got_c
    copies = run(
        [rel_copy(span(chip, x_at(k) * big, big), got_x.at[k - 1], k, x_dev(k)) for k in (1, 2, 3)]
        + [
            rel_copy(span(chip, n_quarter + y_at(k) * big, big), got_y.at[k - 1], 3 + k, y_dev(k))
            for k in (1, 2, 3)
        ]
    )
    scatter_sources()
    finish(copies)

    def sum_of(ref, at, size, arrived):
        value = ref[pl.ds(pl.multiple_of(at, 16), size), :].astype(F32)
        for k in range(arrived.shape[0]):
            value += arrived[k].astype(F32)
        return value.astype(BF16)

    sum_x[...] = sum_of(chip, x * big, big, got_x)
    sum_y[...] = sum_of(chip, n_quarter + y * big, big, got_y)
    copies = run(
        [rel_copy(span(sum_x, y_at(k) * small, small), got_y2.at[k - 1], 6 + k, y_dev(k)) for k in (1, 2, 3)]
        + [rel_copy(span(sum_y, x_at(k) * small, small), got_x2.at[k - 1], 9 + k, x_dev(k)) for k in (1, 2, 3)]
    )
    finish(copies)
    last[0:small, :] = sum_of(sum_x, y * small, small, got_y2)
    last[small : 2 * small, :] = sum_of(sum_y, x * small, small, got_x2)
    copies = run(
        [rel_copy(span(last, z_at(k) * least, least), got_z.at[k - 1], 12 + k, z_dev(k)) for k in range(1, 8)]
    )
    finish(copies)
    side = z // 4
    at_x = mine + x * big + y * small
    at_y = mine + n_quarter + y * big + x * small
    at_z = at_x + side * (at_y - at_x) + lax.rem(z, 4) * least
    rel_out[pl.ds(pl.multiple_of(at_z, 16), least), :] = sum_of(last, z * least, least, got_z)
    same = lambda at, size: [span(rel_out, at, size)] * 2
    finish(run([rel_copy(*same(at_z, least), 19 + k, z_dev(k)) for k in range(1, 8)]))
    finish(
        run(
            [rel_copy(*same(at_x, small), 26 + k, y_dev(k)) for k in (1, 2, 3)]
            + [rel_copy(*same(at_y, small), 29 + k, x_dev(k)) for k in (1, 2, 3)]
        )
    )
    copies = run(
        [rel_copy(*same(mine + x * big, big), 32 + k, x_dev(k)) for k in (1, 2, 3)]
        + [rel_copy(*same(mine + n_quarter + y * big, big), 35 + k, y_dev(k)) for k in (1, 2, 3)]
    )
    take_grads()
    finish(copies)
    finish(run([rel_copy(*same(mine, n_half), 39, core_dev)]))


def bucket(turn, table, relations, meta, requests, rel_prev, groups, shards, capacity):
    rows, width = table.shape
    n_rel, edges = relations.shape[0], meta.shape[1]
    n_own = 64
    n_neg = shards * n_own
    bf = lambda *shape: pltpu.VMEM(shape + (width,), BF16)
    f32 = lambda *shape: pltpu.VMEM(shape + (width,), F32)
    scratch = [
        pltpu.VMEM(requests.shape, jnp.int32),
        pltpu.VMEM((edges, 8), jnp.int32),
        bf(n_own), bf(n_neg),
        bf(shards * capacity), bf(shards * capacity), bf(shards * capacity),
        bf(n_neg), bf(n_neg),
        bf(edges), f32(edges), bf(edges), f32(edges), bf(edges), bf(edges), bf(edges),
        pltpu.VMEM((width, n_neg), F32),
        bf(n_rel), bf(n_rel),
    ]
    if turn:
        scratch += [
            bf(n_rel), bf(n_rel // 2),
            bf(3, n_rel // 16), bf(3, n_rel // 16), bf(n_rel // 16), bf(n_rel // 16),
            bf(3, n_rel // 64), bf(3, n_rel // 64), bf(n_rel // 32), bf(7, n_rel // 256),
        ]
    scratch += [pltpu.SemaphoreType.DMA((shards,))] * 10 + [pltpu.SemaphoreType.DMA((2,))]
    if turn:
        scratch += [pltpu.SemaphoreType.DMA((40,))] * 2
    out = [
        jax.ShapeDtypeStruct((rows, width), F32),
        jax.ShapeDtypeStruct((n_rel, width), BF16),
    ]
    if turn == 0:
        out.append(jax.ShapeDtypeStruct(requests.shape, jnp.int32))
    args = [table, relations, meta, requests] + ([rel_prev] if turn else [])
    return pl.pallas_call(
        functools.partial(bucket_kernel, turn, groups, shards, edges, capacity),
        out_shape=out,
        in_specs=[pl.BlockSpec(memory_space=pltpu.VMEM)] * len(args),
        out_specs=[pl.BlockSpec(memory_space=pltpu.VMEM)] * len(out),
        scratch_shapes=scratch,
        compiler_params=pltpu.CompilerParams(
            collective_id=turn, has_side_effects=True, vmem_limit_bytes=56 << 20
        ),
        name="bucket_one" if turn else "bucket_zero",
    )(*args)


def one_hot(index, size):
    return (index[:, None] == jnp.arange(size, dtype=jnp.int32)[None, :]).astype(BF16)


def one_hot_t(index, size):
    return (jnp.arange(size, dtype=jnp.int32)[:, None] == index[None, :]).astype(BF16)


def plan(owners, dst_rows, shards, capacity):
    edges = owners.shape[0]
    position = jnp.arange(edges, dtype=jnp.int32)
    chosen = one_hot(owners, shards)
    before = (position[None, :] < position[:, None]).astype(BF16)
    ranks = jnp.sum(dot(before, chosen) * chosen.astype(F32), axis=1).astype(jnp.int32)
    chosen_t = one_hot_t(owners, shards)
    by_rank = one_hot(ranks, LANES)
    upper = dot(chosen_t * (dst_rows // 32).astype(BF16)[None, :], by_rank)
    lower = dot(chosen_t * (dst_rows % 32).astype(BF16)[None, :], by_rank)
    return owners * capacity + ranks, (upper * 32 + lower).astype(jnp.int32)


def per_device(
    entities, row_acc, relations, rel_acc, src_row, rel_id, dst_owner, dst_row, neg_rows, lengths
):
    groups, shards = lax.axis_size("grp"), lax.axis_size("shard")
    edges = src_row.shape[-1]
    capacity = 2 * edges // shards
    metas, requests = [], []
    for turn in range(2):
        slot, request = plan(dst_owner[turn, 0, 0, :, 0], dst_row[turn, 0, 0], shards, capacity)
        live = (jnp.arange(edges, dtype=jnp.int32) < lengths[turn, 0, 0]).astype(jnp.int32)
        metas.append(
            jnp.pad(
                jnp.stack([slot, src_row[turn, 0, 0], live, rel_id[turn, 0, 0]]), ((0, 4), (0, 0))
            )
        )
        named = jnp.pad(neg_rows[turn], ((0, 0), (0, LANES - neg_rows.shape[-1])))
        requests.append(jnp.concatenate([request, named]))
    requests = jnp.pad(jnp.stack(requests, axis=1), ((0, 0), (0, 6), (0, 0)))
    first, rel_part, asked = bucket(
        0, entities.astype(BF16), relations, metas[0], requests, None, groups, shards, capacity
    )
    table_one, accum_one = adagrad(entities, row_acc, first)
    second, rel_total = bucket(
        1, table_one.astype(BF16), relations, metas[1], asked, rel_part, groups, shards, capacity
    )
    table_two, accum_two = adagrad(table_one, accum_one, second)
    new_rel, new_racc = adagrad(relations, rel_acc, rel_total.astype(F32))
    return (table_two, accum_two, new_rel, new_racc)


def solution(mesh):
    in_specs = (
        P(("grp", "shard"), None),
        P(("grp", "shard")),
        P(),
        P(),
        P(None, "grp", "shard", None),
        P(None, "grp", "shard", None),
        P(None, "grp", "shard", None, None),
        P(None, "grp", "shard", None),
        P(None, "grp", "shard"),
        P(None, "grp", "shard"),
    )
    out_specs = (P(("grp", "shard"), None), P(("grp", "shard")), P(), P())
    return jax.shard_map(
        per_device, mesh=mesh, in_specs=in_specs, out_specs=out_specs, check_vma=False
    )
```

time: 886 us -> 231 us (0.26); the launches traced: 875 us -> 230 us
  waiting for transfers between devices: 376 us -> 0 us
  Pallas kernels: 0 us -> 205 us
  blocking collectives: 153 us -> 0 us
  other arithmetic: 155 us -> 14.5 us
  local copies, waits for them, and re-layouts: 87.9 us -> 6.94 us
  starting transfers between devices: 73 us -> 0 us
  between operations: 14.9 us -> 0.83 us
  matrix products: 15.4 us -> 2.61 us
    psum x1 -> x0, waiting for transfers between devices: 268 us -> none  [sum_relations(): return lax.psum(gradient, ('grp', 'shard'))]
    pallas_call x0 -> x2, Pallas kernels: none -> 205 us  [bucket(): pl.pallas_call(functools.partial(bucket_kernel, turn, groups, shards, edg...]
    all_gather x2 -> x0, blocking collectives: 153 us -> none  [bucket(): negatives = lax.all_gather(own_negs, 'shard', axis=0, tiled=True)]
    scatter-add x8 -> x0, other arithmetic: 88.2 us -> none  [the longest x4 37.3 us: bucket(): zero_rows.at[asked.reshape(-1)].add(incoming.reshape(-1, width))]
    gather x10 -> x0, local copies, waits for them, and re-layouts: 67.2 us -> none  [the longest x2 32.7 us: bucket(): dst_emb = fetched[owners, ranks]]
    reduce_scatter x2 -> x0, waiting for transfers between devices: 62.9 us -> none  [bucket(): lax.psum_scatter(lax.dot_general(neg_weight, query_bf, (((0,), (0,)), (()...]
    all_to_all x6 -> x0, starting transfers between devices: 37.7 us -> none  [the longest x2 16.9 us: bucket(): lax.all_to_all(request, 'shard', split_axis=0, concat_axis=0, tiled=True)]
    ppermute x2 -> x0, starting transfers between devices: 35.2 us -> none  [passed_along(): return lax.ppermute(block, axis, route)]
  transfers between devices with their start and end apart: 11 -> 0, of which waited for: 8 -> 0; matrix products, arithmetic and copies ran while one was open for 16% -> 0% of each run, Pallas kernels for 0% -> 0%
where the time goes in v1:
time: 231 us; the launch traced here: 230 us
  Pallas kernels  205 us (89%)
  other arithmetic  14.5 us (6%)
  local copies, waits for them, and re-layouts  6.94 us (3%)
  matrix products  2.61 us (1%)
    pallas_call x2, Pallas kernels, bucket(): pl.pallas_call(functools.partial(bucket_kernel, turn, groups, shards, edg...  205 us
    sub x2, other arithmetic, adagrad(): return (table - LEARN_RATE * gradient / jnp.sqrt(total)[..., None], total)  5.11 us

profile of v1, /device:TPU:1, one launch (start us, length us, event | category | flops | bytes accessed | tf_op | source)
XLA Modules:
  0.0 230.2 jit_solution(13871751375069457043)
XLA Ops:
  0.6 0.7 slice_bitcast_fusion.5
  1.3 1.3 fusion.64
  2.6 0.7 compare_convert_fusion
  3.3 0.7 compare_convert_fusion.1
  4.0 0.7 slice_bitcast_fusion.1
  4.7 0.7 slice_bitcast_fusion
  5.4 0.7 slice_reduce_fusion.1
  6.1 0.7 slice_reduce_fusion.2
  6.9 0.6 fusion.11
  7.5 0.6 fusion.12
  9.7 0.6 pad.18.refs_2_
  10.4 0.6 pad.22.refs_2_
  11.0 0.7 pad.21.refs_3_
  11.7 0.8 convert_element_type.115.refs_0_
  12.5 91.7 %bucket_zero.1 = (f32[1024,256]{1,0:T(8,128)}, bf16[4096,256]{1,0:T(8,128)(2,1)}, s32[17,8,256]{2,1,0:T(8,128)}) custom-call(bf16[1024,256]{1,0:T(8,128)(2,1)} %convert_element_type.115.refs_0_, f32[4096,256]{1,0:T(8,128)} %refs_1_.3, s32[8,1152]{1,0:T(8,128)} %pad.18.refs_2_, s32[17,8,256]{2,1,0:T(8,128)} %pad.21.refs_3_), custom_call_target="tpu_custom_call" | custom-call | tf_op jit(solution)/shard_map/bucket_zero/pallas_call | solution.py:427
  104.2 1.4 multiply_reduce_fusion.1
  105.7 2.2 fusion.61.refs_0_
  107.9 113.7 %bucket_one.1 = (f32[1024,256]{1,0:T(8,128)}, bf16[4096,256]{1,0:T(8,128)(2,1)}) custom-call(bf16[1024,256]{1,0:T(8,128)(2,1)} %fusion.61.refs_0_, f32[4096,256]{1,0:T(8,128)} %refs_1_.3, s32[8,1152]{1,0:T(8,128)} %pad.22.refs_2_, s32[17,8,256]{2,1,0:T(8,128)} %get-tuple-element.10.refs_3_, bf16[4096,256]{1,0:T(8,128)(2,1)} %get-tuple-element.11.refs_4_), custom_call_target="tpu_custom_call" | custom-call | tf_op jit(solution)/shard_map/bucket_one/pallas_call | solution.py:427
  221.6 1.6 multiply_reduce_fusion
  223.2 0.6 fusion.63
  223.8 2.7 %divide_subtract_fusion = f32[1024,256]{1,0:T(8,128)} fusion(f32[1024,256]{1,0:T(8,128)} %get-tuple-element.12, f32[1024]{0:T(1024)S(1)} %get-tuple-element.20, f32[1024,256]{1,0:T(8,128)S(1)} %copy-done.1, f32[1024]{0:T(1024)S(1)} %fusion.56, f32[1024,256]{1,0:T(8,128)S(1)} %copy-done.2), kind=kLoop, calls=%fused_computation.24 | loop fusion | flops 1572864 | bytes 4202496 | tf_op jit(solution)/shard_map/sub | solution.py:18
  226.5 0.6 fusion.4
  227.2 0.6 fusion.62
  227.8 2.4 %fusion.3 = f32[4096,256]{1,0:T(8,128)} fusion(f32[4096,256]{1,0:T(8,128)S(1)} %copy-done, bf16[4096,256]{1,0:T(8,128)(2,1)S(1)} %copy-done.3, f32[4096]{0:T(1024)S(1)} %get-tuple-element.18), kind=kLoop, calls=%fused_computation.6 | loop fusion | flops 4194304 | bytes 10502144 | tf_op jit(solution)/shard_map/sub | solution.py:18
  (29 shorter events, 1.8 us)
Async XLA Ops:
  0.6 7.4 %copy-start.4 = (s32[2,1,1,1152,1]{3,4,2,1,0:T(1,128)S(1)}, s32[2,1,1,1152,1]{3,4,2,1,0:T(1,128)}, u32[]{:S(2)}) copy-start(s32[2,1,1,1152,1]{3,4,2,1,0:T(1,128)} %param.16) | copy-start | bytes 27652
  7.4 4.2 %copy-start.1 = (f32[1024,256]{1,0:T(8,128)S(1)}, f32[1024,256]{1,0:T(8,128)}, u32[]{:S(2)}) copy-start(f32[1024,256]{1,0:T(8,128)} %param.10) | copy-start | bytes 3145732
  12.5 93.1 %copy-start.5 = (f32[1024]{0:T(1024)S(1)}, f32[1024]{0:T(1024)}, u32[]{:S(2)}) copy-start(f32[1024]{0:T(1024)} %param.11) | copy-start | bytes 12292
  107.9 115.9 %copy-start.2 = (f32[1024,256]{1,0:T(8,128)S(1)}, f32[1024,256]{1,0:T(8,128)}, u32[]{:S(2)}) copy-start(f32[1024,256]{1,0:T(8,128)} %get-tuple-element.9) | copy-start | bytes 3145732
  221.6 4.9 %copy-start.3 = (bf16[4096,256]{1,0:T(8,128)(2,1)S(1)}, bf16[4096,256]{1,0:T(8,128)(2,1)}, u32[]{:S(2)}) copy-start(bf16[4096,256]{1,0:T(8,128)(2,1)} %get-tuple-element.13) | copy-start | bytes 6291460
  223.8 4.0 %copy-start = (f32[4096,256]{1,0:T(8,128)S(1)}, f32[4096,256]{1,0:T(8,128)}, u32[]{:S(2)}) copy-start(f32[4096,256]{1,0:T(8,128)} %refs_1_.3) | copy-start | bytes 12582916
  226.5 0.7 copy-start.6

commit v2 on v0

v2 whole, which is shorter than its diff:
```python
import functools
import jax
import jax.numpy as jnp
from jax import lax
from jax.experimental import pallas as pl
from jax.experimental.pallas import tpu as pltpu
from jax.sharding import PartitionSpec as P

LEARN_RATE = 0.3
MESH = pl.DeviceIdType.MESH
F32 = jnp.float32
BF16 = jnp.bfloat16
LANES = 256


def adagrad(table, accum, gradient):
    total = accum + jnp.mean(gradient * gradient, axis=-1)
    return (table - LEARN_RATE * gradient / jnp.sqrt(total)[..., None], total)


def dot(a, b):
    return jnp.dot(a, b, preferred_element_type=F32)


def hot(index, size):
    places = lax.broadcasted_iota(jnp.int32, (index.shape[0], size), 1)
    return jnp.where(places == index, 1.0, 0.0).astype(BF16)


def hot_t(index, size, first=0):
    places = lax.broadcasted_iota(jnp.int32, (size, index.shape[1]), 0) + first
    return jnp.where(places == index, 1.0, 0.0).astype(BF16)


def train_kernel(groups, shards, edges, capacity, n_own, *refs):
    (entities, row_acc, relations, src_row, rel_id, dst_owner, dst_row, neg_rows, lengths,
     table, acc_out, rel_out,
     meta, meta_t, requests, asked, asked_next, asked_t, chunks, high, low, table_bf, acc_t,
     own_negs, negs_2, sent, got_2, back_2, neg_send, pair_got_2, pair_sum, neg_got_2,
     src_emb, rel_rows_2, query_bf, query_grad, src_grad, rel_grad, dst_grad, neg_acc, total,
     by_slot, by_slot_t, by_asked_t, by_rel_t,
     half, rel_got_c, got_x, got_y, sum_x, sum_y, got_x2, got_y2, last, got_z,
     chunk_sem, req_send, req_recv, neg_sems, row_send, row_recv, pair_sems,
     ngr_send, ngr_recv, grad_send, grad_recv, next_sem, rel_send, rel_recv) = refs

    rows, width = table.shape
    n_rel = relations.shape[0]
    n_neg = shards * n_own
    n_side = n_neg // 2
    depth = shards // 2
    slots = shards * capacity
    g, s = lax.axis_index("grp"), lax.axis_index("shard")
    next_g, prev_g = lax.rem(g + 1, groups), lax.rem(g + groups - 1, groups)
    tile = edges // 3
    chunk = lambda ref, i, size: ref.at[pl.ds(pl.multiple_of(i * size, 16), size)]
    span = lambda ref, at, size: ref.at[pl.ds(pl.multiple_of(at, 16), size)]

    x, y_hi, core = g // 4, lax.rem(g // 2, 2), lax.rem(g, 2)
    z, y_lo = s // 2, lax.rem(s, 2)
    y = y_hi * 2 + y_lo
    pair_s = z * 2 + 1 - y_lo
    along = lambda k: lax.rem(z + k, depth) * 2 + y_lo

    def device(x, y, z, core):
        return (x * 4 + (y // 2) * 2 + core, z * 2 + lax.rem(y, 2))

    x_at = lambda k: lax.rem(x + k, 4)
    y_at = lambda k: lax.rem(y + k, 4)
    z_at = lambda k: lax.rem(z + k, 8)
    x_dev = lambda k: device(x_at(k), y, z, core)
    y_dev = lambda k: device(x, y_at(k), z, core)
    z_dev = lambda k: device(x, y, z_at(k), core)
    core_dev = device(x, y, z, 1 - core)

    def each(begin, end, body):
        def step(k, carry):
            body(k)
            return carry

        lax.fori_loop(begin, end, step, 0)

    barrier = pltpu.get_barrier_semaphore()

    def greet(where):
        pl.semaphore_signal(barrier, inc=1, device_id=where, device_id_type=MESH)

    each(1, shards, lambda k: greet((g, lax.rem(s + shards - k, shards))))
    others = [(prev_g, s), core_dev] + [x_dev(k) for k in (1, 2, 3)] + [y_dev(k) for k in (1, 2, 3)]
    for other in others:
        greet(other)

    rel_steps = n_rel // chunks.shape[1]

    def load(i):
        return pltpu.make_async_copy(
            chunk(relations, i, chunks.shape[1]), chunks.at[i % 2], chunk_sem.at[i % 2]
        )

    load(0).start()
    load(1).start()

    for t in range(2):
        meta[t : t + 1, :] = dst_owner[t, 0]
        meta[2 + t : 3 + t, :] = src_row[t, 0]
        meta[4 + t : 5 + t, :] = rel_id[t, 0]
    meta[6:8, :] = jnp.zeros((2, edges), jnp.int32)
    meta_t[...] = jnp.transpose(meta[...])
    requests[...] = jnp.zeros_like(requests)
    lower_tri = jnp.where(
        lax.broadcasted_iota(jnp.int32, (128, 128), 1)
        < lax.broadcasted_iota(jnp.int32, (128, 128), 0),
        1.0,
        0.0,
    ).astype(BF16)
    shard_rows = lax.broadcasted_iota(jnp.int32, (shards, 128), 0)
    for t in range(2):
        base = jnp.zeros((1, 128), F32)
        upper = jnp.zeros((shards, LANES), F32)
        lower = jnp.zeros((shards, LANES), F32)
        for b in range(edges // 128):
            at = slice(b * 128, b * 128 + 128)
            owner = meta_t[at, t : t + 1]
            chosen = hot(owner, 128)
            chosen_f = chosen.astype(F32)
            count = dot(lower_tri, chosen) + base
            rank = jnp.sum(count * chosen_f, axis=1, keepdims=True).astype(jnp.int32)
            base = base + jnp.sum(chosen_f, axis=0, keepdims=True)
            meta_t[at, 6 + t : 7 + t] = owner * capacity + rank
            by_rank = hot(rank, LANES)
            row = dst_row[t, 0, :, at]
            named = meta[t : t + 1, at] == shard_rows
            part = lambda value: dot(jnp.where(named, value.astype(F32), 0.0).astype(BF16), by_rank)
            upper = upper + part(lax.shift_right_logical(row, 5))
            lower = lower + part(row & 31)
        asking = (upper * 32.0 + lower).astype(jnp.int32)
        for o in range(shards):
            requests[o, t : t + 1, :] = asking[o : o + 1, :]
        requests[shards, t : t + 1, :n_own] = neg_rows[t]
    meta[...] = jnp.transpose(meta_t[...])
    table[...] = entities[...]
    table_bf[...] = entities[...].astype(BF16)
    acc_t[...] = jnp.transpose(row_acc[...])

    def name_negatives(t):
        column = jnp.transpose((asked_next if t else requests)[shards])[:n_own, t : t + 1]
        own_negs[...] = dot(hot(column, rows), table_bf[...]).astype(BF16)

    name_negatives(0)
    pl.semaphore_wait(barrier, shards - 1 + len(others))

    def request_copy(k):
        target = lax.rem(s + k, shards)
        return pltpu.make_async_remote_copy(
            src_ref=requests.at[target], dst_ref=asked.at[s],
            send_sem=req_send.at[k], recv_sem=req_recv.at[k],
            device_id=(g, target), device_id_type=MESH,
        )

    forward = pltpu.make_async_remote_copy(
        src_ref=asked, dst_ref=asked_next, send_sem=next_sem.at[0], recv_sem=next_sem.at[1],
        device_id=(next_g, s), device_id_type=MESH,
    )

    def look_relations(t):
        def step(i, carry):
            at = pl.ds(pl.multiple_of(i * tile, 128), tile)
            picked = hot(meta_t[at, :][:, 4 + t : 5 + t], n_rel)
            rel_rows_2[t, at, :] = dot(picked, high[...]) + dot(picked, low[...])
            return carry

        lax.fori_loop(0, 3, step, 0)

    def round_of(t):
        to_g = prev_g if t else g
        from_g = next_g if t else g
        first = 0 if t else 1
        negs, got, back = negs_2.at[t], got_2.at[t], back_2.at[t]
        pair_got, neg_got, rel_rows = pair_got_2.at[t], neg_got_2.at[t], rel_rows_2.at[t]
        wanted = asked_next if t else asked
        limit = lengths[t, 0, 0]

        def live(i):
            place = lax.broadcasted_iota(jnp.int32, (tile, 1), 0) + i * tile
            return place < limit

        my_block = y_lo * depth + z

        def neg_copy(k):
            return pltpu.make_async_remote_copy(
                src_ref=own_negs, dst_ref=chunk(negs, my_block, n_own),
                send_sem=neg_sems.at[t, 0, k], recv_sem=neg_sems.at[t, 1, k],
                device_id=(to_g, along(k)), device_id_type=MESH,
            )

        neg_pair = pltpu.make_async_remote_copy(
            src_ref=chunk(negs, y_lo, n_side), dst_ref=chunk(negs, y_lo, n_side),
            send_sem=neg_sems.at[t, 0, depth], recv_sem=neg_sems.at[t, 1, depth],
            device_id=(g, pair_s), device_id_type=MESH,
        )

        def row_copy(k):
            target = lax.rem(s + k, shards)
            return pltpu.make_async_remote_copy(
                src_ref=chunk(sent, target, capacity), dst_ref=chunk(got, s, capacity),
                send_sem=row_send.at[t, k], recv_sem=row_recv.at[t, k],
                device_id=(to_g, target), device_id_type=MESH,
            )

        pair_copy = pltpu.make_async_remote_copy(
            src_ref=chunk(neg_send, 1 - y_lo, n_side), dst_ref=pair_got,
            send_sem=pair_sems.at[t, 0], recv_sem=pair_sems.at[t, 1],
            device_id=(g, pair_s), device_id_type=MESH,
        )

        def neg_grad_copy(k):
            return pltpu.make_async_remote_copy(
                src_ref=chunk(pair_sum, z_at(k), n_own), dst_ref=chunk(neg_got, z, n_own),
                send_sem=ngr_send.at[t, k], recv_sem=ngr_recv.at[t, k],
                device_id=(from_g, along(k)), device_id_type=MESH,
            )

        def grad_copy(k):
            target = lax.rem(s + k, shards)
            return pltpu.make_async_remote_copy(
                src_ref=chunk(sent, target, capacity), dst_ref=chunk(back, s, capacity),
                send_sem=grad_send.at[t, k], recv_sem=grad_recv.at[t, k],
                device_id=(from_g, target), device_id_type=MESH,
            )

        if t == 0:
            each(1, shards, lambda k: request_copy(k).start())
            asked[s] = requests[s]
            asked[shards] = requests[shards]
            negs[pl.ds(pl.multiple_of(my_block * n_own, 16), n_own), :] = own_negs[...]
        else:
            forward.wait()
            name_negatives(1)
        each(first, depth, lambda k: neg_copy(k).start())

        if t == 0:
            for i in range(rel_steps):
                load(i).wait()
                value = chunks[i % 2]
                top = value.astype(BF16)
                at = slice(i * chunks.shape[1], (i + 1) * chunks.shape[1])
                high[at, :] = top
                low[at, :] = (value - top.astype(F32)).astype(BF16)
                if i + 2 < rel_steps:
                    load(i + 2).start()
            each(1, shards, lambda k: request_copy(k).wait())
            forward.start()

        def answer(who):
            columns = jnp.transpose(wanted[who])[:capacity, :]
            asked_t[pl.ds(pl.multiple_of(who * capacity, 16), capacity), :] = columns
            return dot(hot(columns[:, t : t + 1], rows), table_bf[...]).astype(BF16)

        def send_rows(k):
            target = lax.rem(s + k, shards)
            sent[pl.ds(pl.multiple_of(target * capacity, 16), capacity), :] = answer(target)
            row_copy(k).start()

        each(first, shards, send_rows)
        if t == 0:
            got[pl.ds(pl.multiple_of(s * capacity, 16), capacity), :] = answer(s)
        each(first, depth, lambda k: neg_copy(k).wait())
        neg_pair.start()

        if t == 0:
            look_relations(0)

        def look_sources(i, carry):
            at = pl.ds(pl.multiple_of(i * tile, 128), tile)
            emb = dot(hot(meta_t[at, :][:, 2 + t : 3 + t], rows), table_bf[...])
            src_emb[at, :] = emb.astype(BF16)
            query_bf[at, :] = (emb * rel_rows[at, :]).astype(BF16)
            return carry

        lax.fori_loop(0, 3, look_sources, 0)

        neg_pair.wait()
        neg_acc[...] = jnp.zeros_like(neg_acc)

        def against_negatives(i, carry):
            at = pl.ds(pl.multiple_of(i * tile, 128), tile)
            query = query_bf[at, :]
            scores = lax.dot_general(
                query, negs[...], (((1,), (1,)), ((), ())), preferred_element_type=F32
            )
            weight = jnp.where(
                live(i), (jnp.tanh(scores * 0.5) + 1.0) * (0.5 / n_neg), 0.0
            ).astype(BF16)
            query_grad[at, :] = dot(weight, negs[...])
            neg_acc[...] += dot(jnp.transpose(query.astype(F32)).astype(BF16), weight)
            return carry

        lax.fori_loop(0, 3, against_negatives, 0)
        neg_send[...] = jnp.transpose(neg_acc[...]).astype(BF16)
        pair_copy.start()

        def mark_slots(i):
            at = pl.ds(pl.multiple_of(i * 128, 128), 128)
            by_slot[at, :] = hot(meta_t[at, :][:, 6 + t : 7 + t], slots)

        each(0, edges // 128, mark_slots)

        pair_copy.wait()
        mine_side = pl.ds(pl.multiple_of(y_lo * n_side, 16), n_side)
        pair_sum[...] = (neg_send[mine_side, :].astype(F32) + pair_got[...].astype(F32)).astype(BF16)
        if t == 0:
            own = pl.ds(pl.multiple_of(z * n_own, 16), n_own)
            neg_got[own, :] = pair_sum[own, :]
        each(first, depth, lambda k: neg_grad_copy(k).start())

        def mark_slots_t(i):
            at = pl.multiple_of(i * 128, 128)
            by_slot_t[pl.ds(at, 128), :] = hot_t(meta[6 + t : 7 + t, :], 128, at)

        each(0, slots // 128, mark_slots_t)
        asked_rows = jnp.transpose(asked_t[...])[t : t + 1, :]

        def mark_asked(i):
            at = pl.multiple_of(i * 128, 128)
            by_asked_t[pl.ds(at, 128), :] = hot_t(asked_rows, 128, at)

        each(0, rows // 128, mark_asked)

        n_half, n_quarter = n_rel // 2, n_rel // 4
        mine, theirs = core * n_half, (1 - core) * n_half
        if t:

            def mark_relations(i):
                at = pl.multiple_of(i * 128, 128)
                by_rel_t[pl.ds(at, 128), :] = hot_t(meta[4 + t : 5 + t, :], 128, theirs + at)

            each(0, n_half // 128, mark_relations)

        each(first, shards, lambda k: row_copy(k).wait_recv())

        def positives(i, carry):
            at = pl.ds(pl.multiple_of(i * tile, 128), tile)
            emb = src_emb[at, :].astype(F32)
            rel = rel_rows[at, :]
            query = emb * rel
            dst = dot(by_slot[at, :], got[...])
            positive = jnp.sum(query * dst, axis=1, keepdims=True)
            weight = jnp.where(live(i), (jnp.tanh(positive * -0.5) + 1.0) * -0.5, 0.0)
            grad = weight * dst + query_grad[at, :]
            src_grad[at, :] = (grad * rel).astype(BF16)
            rel_grad[at, :] = (grad * emb).astype(BF16)
            dst_grad[at, :] = (weight * query).astype(BF16)
            return carry

        lax.fori_loop(0, 3, positives, 0)

        def send_grads():
            each(first, shards, lambda k: row_copy(k).wait_send())

            def block(target):
                at = pl.ds(pl.multiple_of(target * capacity, 16), capacity)
                return dot(by_slot_t[at, :], dst_grad[...]).astype(BF16)

            def send(k):
                target = lax.rem(s + k, shards)
                sent[pl.ds(pl.multiple_of(target * capacity, 16), capacity), :] = block(target)
                grad_copy(k).start()

            each(first, shards, send)
            if t == 0:
                back[pl.ds(pl.multiple_of(s * capacity, 16), capacity), :] = block(s)

        def scatter_sources():
            def step(i):
                at = pl.multiple_of(i * 256, 256)
                total[pl.ds(at, 256), :] = dot(hot_t(meta[2 + t : 3 + t, :], 256, at), src_grad[...])

            each(0, rows // 256, step)

        def take_grads():
            each(first, depth, lambda k: neg_grad_copy(k).wait())
            summed = neg_got[0:n_own, :].astype(F32)
            for k in range(1, depth):
                summed += neg_got[k * n_own : (k + 1) * n_own, :].astype(F32)
            upper = summed.astype(BF16)
            lower = (summed - upper.astype(F32)).astype(BF16)
            picked = hot_t(wanted[shards][t : t + 1, :n_own], rows)
            total[...] += dot(picked, upper) + dot(picked, lower)
            each(first, shards, lambda k: grad_copy(k).wait())
            for i in range(rows // 128):
                at = slice(i * 128, i * 128 + 128)
                grad = total[at, :] + dot(by_asked_t[at, :], back[...])
                acc = acc_t[:, i : i + 1] + jnp.sum(grad * grad, axis=1, keepdims=True) * (1.0 / width)
                fresh = table[at, :] - LEARN_RATE * grad / jnp.sqrt(acc)
                acc_t[:, i : i + 1] = acc
                table[at, :] = fresh
                if t == 0:
                    table_bf[at, :] = fresh.astype(BF16)

        if t == 0:
            send_grads()
            scatter_sources()

            def scatter(i):
                at = pl.multiple_of(i * 512, 512)
                part = dot(hot_t(meta[4:5, :], 512, at), rel_grad[...])
                half[pl.ds(at, 512), :] = part.astype(BF16)

            each(0, n_rel // 512, scatter)
            look_relations(1)
            take_grads()
            return

        big, small, least = n_quarter // 4, n_quarter // 16, n_rel // 256

        def rel_copy(src, dst, sem, where):
            return pltpu.make_async_remote_copy(
                src_ref=src, dst_ref=dst, send_sem=rel_send.at[sem], recv_sem=rel_recv.at[sem],
                device_id=where, device_id_type=MESH,
            )

        def run(copies):
            for copy in copies:
                copy.start()
            return copies

        def finish(copies):
            for copy in copies:
                copy.wait()

        def scatter_theirs(i):
            at = pl.multiple_of(i * 512, 512)
            where = pl.ds(pl.multiple_of(theirs + at, 512), 512)
            part = dot(by_rel_t[pl.ds(at, 512), :], rel_grad[...])
            half[where, :] = (half[where, :].astype(F32) + part).astype(BF16)

        def scatter_mine(i):
            at = pl.multiple_of(mine + i * 512, 512)
            part = dot(hot_t(meta[5:6, :], 512, at), rel_grad[...])
            half[pl.ds(at, 512), :] = (half[pl.ds(at, 512), :].astype(F32) + part).astype(BF16)

        each(0, n_half // 512, scatter_theirs)
        copies = run([rel_copy(span(half, theirs, n_half), rel_got_c, 0, core_dev)])
        send_grads()
        each(0, n_half // 512, scatter_mine)
        finish(copies)

        def add_core(i):
            at = pl.multiple_of(i * 256, 256)
            mine_at = pl.ds(pl.multiple_of(mine + at, 256), 256)
            value = half[mine_at, :].astype(F32) + rel_got_c[pl.ds(at, 256), :].astype(F32)
            rel_got_c[pl.ds(at, 256), :] = value.astype(BF16)

        each(0, n_half // 256, add_core)
        chip = rel_got_c
        copies = run(
            [rel_copy(span(chip, x_at(k) * big, big), got_x.at[k - 1], k, x_dev(k)) for k in (1, 2, 3)]
            + [
                rel_copy(span(chip, n_quarter + y_at(k) * big, big), got_y.at[k - 1], 3 + k, y_dev(k))
                for k in (1, 2, 3)
            ]
        )
        scatter_sources()
        finish(copies)

        def sum_of(ref, at, size, arrived):
            value = ref[pl.ds(pl.multiple_of(at, 16), size), :].astype(F32)
            for k in range(arrived.shape[0]):
                value += arrived[k].astype(F32)
            return value.astype(BF16)

        sum_x[...] = sum_of(chip, x * big, big, got_x)
        sum_y[...] = sum_of(chip, n_quarter + y * big, big, got_y)
        copies = run(
            [rel_copy(span(sum_x, y_at(k) * small, small), got_y2.at[k - 1], 6 + k, y_dev(k)) for k in (1, 2, 3)]
            + [rel_copy(span(sum_y, x_at(k) * small, small), got_x2.at[k - 1], 9 + k, x_dev(k)) for k in (1, 2, 3)]
        )
        finish(copies)
        last[0:small, :] = sum_of(sum_x, y * small, small, got_y2)
        last[small : 2 * small, :] = sum_of(sum_y, x * small, small, got_x2)
        copies = run(
            [rel_copy(span(last, z_at(k) * least, least), got_z.at[k - 1], 12 + k, z_dev(k)) for k in range(1, 8)]
        )
        finish(copies)
        side = z // 4
        at_x = mine + x * big + y * small
        at_y = mine + n_quarter + y * big + x * small
        at_z = at_x + side * (at_y - at_x) + lax.rem(z, 4) * least
        rel_out[pl.ds(pl.multiple_of(at_z, 16), least), :] = sum_of(last, z * least, least, got_z)
        same = lambda at, size: [span(rel_out, at, size)] * 2
        finish(run([rel_copy(*same(at_z, least), 19 + k, z_dev(k)) for k in range(1, 8)]))
        finish(
            run(
                [rel_copy(*same(at_x, small), 26 + k, y_dev(k)) for k in (1, 2, 3)]
                + [rel_copy(*same(at_y, small), 29 + k, x_dev(k)) for k in (1, 2, 3)]
            )
        )
        copies = run(
            [rel_copy(*same(mine + x * big, big), 32 + k, x_dev(k)) for k in (1, 2, 3)]
            + [rel_copy(*same(mine + n_quarter + y * big, big), 35 + k, y_dev(k)) for k in (1, 2, 3)]
        )
        finish(copies)
        copies = run([rel_copy(*same(mine, n_half), 39, core_dev)])
        take_grads()
        finish(copies)

    round_of(0)
    round_of(1)
    acc_out[...] = jnp.transpose(acc_t[...])


def train(entities, row_acc, relations, src_row, rel_id, dst_owner, dst_row, neg_rows, lengths):
    groups, shards = lax.axis_size("grp"), lax.axis_size("shard")
    rows, width = entities.shape
    n_rel, edges, n_own = relations.shape[0], src_row.shape[-1], neg_rows.shape[-1]
    capacity = 2 * edges // shards
    n_neg, slots, depth = shards * n_own, shards * capacity, shards // 2
    bf = lambda *shape: pltpu.VMEM(shape + (width,), BF16)
    f32 = lambda *shape: pltpu.VMEM(shape + (width,), F32)
    i32 = lambda *shape: pltpu.VMEM(shape, jnp.int32)
    sems = lambda *shape: pltpu.SemaphoreType.DMA(shape)
    scratch = [
        i32(8, edges), i32(edges, 8),
        i32(shards + 1, 8, LANES), i32(shards + 1, 8, LANES), i32(shards + 1, 8, LANES), i32(slots, 8),
        f32(2, 512), bf(n_rel), bf(n_rel), bf(rows), pltpu.VMEM((rows // 8, 8), F32),
        bf(n_own), bf(2, n_neg), bf(slots), bf(2, slots), bf(2, slots),
        bf(n_neg), bf(2, n_neg // 2), bf(n_neg // 2), bf(2, n_neg // 2),
        bf(edges), f32(2, edges), bf(edges), f32(edges), bf(edges), bf(edges), bf(edges),
        pltpu.VMEM((width, n_neg), F32), f32(rows),
        pltpu.VMEM((edges, slots), BF16), pltpu.VMEM((slots, edges), BF16),
        pltpu.VMEM((rows, slots), BF16), pltpu.VMEM((n_rel // 2, edges), BF16),
        bf(n_rel), bf(n_rel // 2),
        bf(3, n_rel // 16), bf(3, n_rel // 16), bf(n_rel // 16), bf(n_rel // 16),
        bf(3, n_rel // 64), bf(3, n_rel // 64), bf(n_rel // 32), bf(7, n_rel // 256),
        sems(2), sems(shards), sems(shards), sems(2, 2, depth + 1),
        sems(2, shards), sems(2, shards), sems(2, 2),
        sems(2, depth), sems(2, depth), sems(2, shards), sems(2, shards),
        sems(2), sems(40), sems(40),
    ]
    vmem = pl.BlockSpec(memory_space=pltpu.VMEM)
    return pl.pallas_call(
        functools.partial(train_kernel, groups, shards, edges, capacity, n_own),
        out_shape=[
            jax.ShapeDtypeStruct((rows, width), F32),
            jax.ShapeDtypeStruct((8, rows // 8), F32),
            jax.ShapeDtypeStruct((n_rel, width), BF16),
        ],
        in_specs=[vmem, vmem, pl.BlockSpec(memory_space=pl.ANY)] + [vmem] * 5
        + [pl.BlockSpec(memory_space=pltpu.SMEM)],
        out_specs=[vmem] * 3,
        scratch_shapes=scratch,
        compiler_params=pltpu.CompilerParams(
            collective_id=0, has_side_effects=True, vmem_limit_bytes=60 << 20
        ),
        name="train",
    )(
        entities, row_acc.reshape(8, rows // 8), relations, src_row, rel_id,
        dst_owner[..., 0], dst_row, neg_rows, lengths,
    )


def per_device(
    entities, row_acc, relations, rel_acc, src_row, rel_id, dst_owner, dst_row, neg_rows, lengths
):
    table, accum, rel_total = train(
        entities, row_acc, relations, src_row, rel_id, dst_owner, dst_row, neg_rows, lengths
    )
    new_rel, new_racc = adagrad(relations, rel_acc, rel_total.astype(F32))
    return (table, accum.reshape(-1), new_rel, new_racc)


def solution(mesh):
    in_specs = (
        P(("grp", "shard"), None),
        P(("grp", "shard")),
        P(),
        P(),
        P(None, "grp", "shard", None),
        P(None, "grp", "shard", None),
        P(None, "grp", "shard", None, None),
        P(None, "grp", "shard", None),
        P(None, "grp", "shard"),
        P(None, "grp", "shard"),
    )
    out_specs = (P(("grp", "shard"), None), P(("grp", "shard")), P(), P())
    return jax.shard_map(
        per_device, mesh=mesh, in_specs=in_specs, out_specs=out_specs, check_vma=False
    )
```

time: 886 us -> 202 us (0.23); the launches traced: 875 us -> 201 us
  waiting for transfers between devices: 376 us -> 0 us
  Pallas kernels: 0 us -> 190 us
  blocking collectives: 153 us -> 0 us
  other arithmetic: 155 us -> 7.39 us
  local copies, waits for them, and re-layouts: 87.9 us -> 2.88 us
  starting transfers between devices: 73 us -> 0 us
  matrix products: 15.4 us -> 0 us
  between operations: 14.9 us -> 0.67 us
    psum x1 -> x0, waiting for transfers between devices: 268 us -> none  [sum_relations(): return lax.psum(gradient, ('grp', 'shard'))]
    pallas_call x0 -> x1, Pallas kernels: none -> 190 us  [train(): pl.pallas_call(functools.partial(train_kernel, groups, shards, edges, cap...]
    all_gather x2 -> x0, blocking collectives: 153 us -> none  [bucket(): negatives = lax.all_gather(own_negs, 'shard', axis=0, tiled=True)]
    scatter-add x8 -> x0, other arithmetic: 88.2 us -> none  [the longest x4 37.3 us: bucket(): zero_rows.at[asked.reshape(-1)].add(incoming.reshape(-1, width))]
    gather x10 -> x0, local copies, waits for them, and re-layouts: 67.2 us -> none  [the longest x2 32.7 us: bucket(): dst_emb = fetched[owners, ranks]]
    reduce_scatter x2 -> x0, waiting for transfers between devices: 62.9 us -> none  [bucket(): lax.psum_scatter(lax.dot_general(neg_weight, query_bf, (((0,), (0,)), (()...]
    all_to_all x6 -> x0, starting transfers between devices: 37.7 us -> none  [the longest x2 16.9 us: bucket(): lax.all_to_all(request, 'shard', split_axis=0, concat_axis=0, tiled=True)]
    ppermute x2 -> x0, starting transfers between devices: 35.2 us -> none  [passed_along(): return lax.ppermute(block, axis, route)]
  transfers between devices with their start and end apart: 11 -> 0, of which waited for: 8 -> 0; matrix products, arithmetic and copies ran while one was open for 16% -> 0% of each run, Pallas kernels for 0% -> 0%
where the time goes in v2:
time: 202 us; the launch traced here: 201 us
  Pallas kernels  190 us (94%)
  other arithmetic  7.39 us (4%)
  local copies, waits for them, and re-layouts  2.88 us (1%)
    pallas_call x1, Pallas kernels, train(): pl.pallas_call(functools.partial(train_kernel, groups, shards, edges, cap...  190 us
    sub x1, other arithmetic, adagrad(): return (table - LEARN_RATE * gradient / jnp.sqrt(total)[..., None], total)  4.57 us

profile of v2, /device:TPU:1, one launch (start us, length us, event | category | flops | bytes accessed | tf_op | source)
XLA Modules:
  0.0 201.3 jit_solution(7529646156979481040)
XLA Ops:
  0.6 0.0 copy-start.1
  0.6 1.3 copy.14.refs_8_
  1.9 190.4 %train.1 = (f32[1024,256]{1,0:T(8,128)}, f32[8,128]{1,0:T(8,128)}, bf16[4096,256]{1,0:T(8,128)(2,1)}) custom-call(f32[1024,256]{1,0:T(8,128)} %refs_0_.1, f32[8,128]{1,0:T(8,128)} %bitcast.4, f32[4096,256]{1,0:T(8,128)} %refs_2_.1, s32[2,1,1,1152]{3,2,1,0:T(1,128)} %refs_3_.1, s32[2,1,1,1152]{3,2,1,0:T(1,128)} %refs_4_.1, s32[2,1,1,1152]{3,2,1,0:T(1,128)} %bitcast.3, ...), custom_call_target="tpu_custom_call" | custom-call | tf_op jit(solution)/shard_map/train/pallas_call | solution.py:540
  192.4 2.2 %fusion.2 = f32[4096]{0:T(1024)S(1)} fusion(bf16[4096,256]{1,0:T(8,128)(2,1)} %get-tuple-element.9), kind=kLoop, calls=%fused_computation.4 | loop fusion | flops 3141632 | bytes 2113536 | tf_op jit(solution)/shard_map/reduce_sum | solution.py:17
  194.6 0.0 copy-done.1
  194.6 0.6 fusion.3
  195.2 0.0 copy-start
  195.2 0.0 copy-start.2
  195.2 4.6 %fusion.1 = f32[4096,256]{1,0:T(8,128)} fusion(f32[4096,256]{1,0:T(8,128)} %refs_2_.1, bf16[4096,256]{1,0:T(8,128)(2,1)} %get-tuple-element.9, f32[4096]{0:T(1024)S(1)} %get-tuple-element.10), kind=kLoop, calls=%fused_computation.3 | loop fusion | flops 4194304 | bytes 10502144 | tf_op jit(solution)/shard_map/sub | solution.py:18
  199.8 0.0 copy-done
  199.8 1.0 copy.17
  200.7 0.0 copy-done.2
  200.7 0.6 copy.18
Async XLA Ops:
  0.6 193.9 %copy-start.1 = (f32[4096]{0:T(1024)S(1)}, f32[4096]{0:T(1024)}, u32[]{:S(2)}) copy-start(f32[4096]{0:T(1024)} %param.13) | copy-start | bytes 49156
  195.2 4.6 %copy-start = (f32[1024,256]{1,0:T(8,128)S(1)}, f32[1024,256]{1,0:T(8,128)}, u32[]{:S(2)}) copy-start(f32[1024,256]{1,0:T(8,128)} %get-tuple-element.16) | copy-start | bytes 3145732
  195.2 5.5 %copy-start.2 = (f32[8,128]{1,0:T(8,128)S(1)}, f32[8,128]{1,0:T(8,128)}, u32[]{:S(2)}) copy-start(f32[8,128]{1,0:T(8,128)} %get-tuple-element.8) | copy-start | bytes 12292

commit v3 on v2

--- a/solution.py
+++ b/solution.py
@@ -35,9 +35,9 @@
 def train_kernel(groups, shards, edges, capacity, n_own, *refs):
     (entities, row_acc, relations, src_row, rel_id, dst_owner, dst_row, neg_rows, lengths,
      table, acc_out, rel_out,
-     meta, meta_t, requests, asked, asked_next, asked_t, chunks, high, low, table_bf, acc_t,
-     own_negs, negs_2, sent, got_2, back_2, neg_send, pair_got_2, pair_sum, neg_got_2,
-     src_emb, rel_rows_2, query_bf, query_grad, src_grad, rel_grad, dst_grad, neg_acc, total,
+     meta, meta_t, requests_2, asked_2, asked_next, asked_t, chunks, high, low, table_bf, acc_t,
+     own_negs, negs_2, sent, queries, got_2, back_2, neg_send, pair_got_2, pair_sum, neg_got_2,
+     src_emb, rel_rows_2, query_bf, query_grad, src_grad, rel_grad, neg_acc, total,
      by_slot, by_slot_t, by_asked_t, by_rel_t,
      half, rel_got_c, got_x, got_y, sum_x, sum_y, got_x2, got_y2, last, got_z,
      chunk_sem, req_send, req_recv, neg_sems, row_send, row_recv, pair_sems,
@@ -99,21 +99,35 @@
     load(0).start()
     load(1).start()
 
+    table[...] = entities[...]
+    table_bf[...] = entities[...].astype(BF16)
+    requests_2[...] = jnp.zeros_like(requests_2)
     for t in range(2):
-        meta[t : t + 1, :] = dst_owner[t, 0]
-        meta[2 + t : 3 + t, :] = src_row[t, 0]
-        meta[4 + t : 5 + t, :] = rel_id[t, 0]
-    meta[6:8, :] = jnp.zeros((2, edges), jnp.int32)
-    meta_t[...] = jnp.transpose(meta[...])
-    requests[...] = jnp.zeros_like(requests)
-    lower_tri = jnp.where(
-        lax.broadcasted_iota(jnp.int32, (128, 128), 1)
-        < lax.broadcasted_iota(jnp.int32, (128, 128), 0),
-        1.0,
-        0.0,
-    ).astype(BF16)
-    shard_rows = lax.broadcasted_iota(jnp.int32, (shards, 128), 0)
-    for t in range(2):
+        requests_2[t, shards, 0:1, :n_own] = neg_rows[t]
+
+    def name_negatives(named):
+        column = jnp.transpose(named[shards])[:n_own, 0:1]
+        own_negs[...] = dot(hot(column, rows), table_bf[...]).astype(BF16)
+
+    name_negatives(requests_2.at[0])
+    pl.semaphore_wait(barrier, shards - 1 + len(others))
+
+    def index_edges():
+        for t in range(2):
+            meta[t : t + 1, :] = dst_owner[t, 0]
+            meta[2 + t : 3 + t, :] = src_row[t, 0]
+            meta[4 + t : 5 + t, :] = rel_id[t, 0]
+        meta[6:8, :] = jnp.zeros((2, edges), jnp.int32)
+        meta_t[...] = jnp.transpose(meta[...])
+
+    def plan(t):
+        lower_tri = jnp.where(
+            lax.broadcasted_iota(jnp.int32, (128, 128), 1)
+            < lax.broadcasted_iota(jnp.int32, (128, 128), 0),
+            1.0,
+            0.0,
+        ).astype(BF16)
+        shard_rows = lax.broadcasted_iota(jnp.int32, (shards, 128), 0)
         base = jnp.zeros((1, 128), F32)
         upper = jnp.zeros((shards, LANES), F32)
         lower = jnp.zeros((shards, LANES), F32)
@@ -134,30 +148,24 @@
             lower = lower + part(row & 31)
         asking = (upper * 32.0 + lower).astype(jnp.int32)
         for o in range(shards):
-            requests[o, t : t + 1, :] = asking[o : o + 1, :]
-        requests[shards, t : t + 1, :n_own] = neg_rows[t]
-    meta[...] = jnp.transpose(meta_t[...])
-    table[...] = entities[...]
-    table_bf[...] = entities[...].astype(BF16)
-    acc_t[...] = jnp.transpose(row_acc[...])
-
-    def name_negatives(t):
-        column = jnp.transpose((asked_next if t else requests)[shards])[:n_own, t : t + 1]
-        own_negs[...] = dot(hot(column, rows), table_bf[...]).astype(BF16)
-
-    name_negatives(0)
-    pl.semaphore_wait(barrier, shards - 1 + len(others))
-
-    def request_copy(k):
+            requests_2[t, o, 0:1, :] = asking[o : o + 1, :]
+
+    def request_copy(t, k):
         target = lax.rem(s + k, shards)
         return pltpu.make_async_remote_copy(
-            src_ref=requests.at[target], dst_ref=asked.at[s],
-            send_sem=req_send.at[k], recv_sem=req_recv.at[k],
+            src_ref=requests_2.at[t, target], dst_ref=asked_2.at[t, s],
+            send_sem=req_send.at[t, k], recv_sem=req_recv.at[t, k],
             device_id=(g, target), device_id_type=MESH,
         )
 
+    def ask(t):
+        plan(t)
+        each(1, shards, lambda k: request_copy(t, k).start())
+        asked_2[t, s] = requests_2[t, s]
+        asked_2[t, shards] = requests_2[t, shards]
+
     forward = pltpu.make_async_remote_copy(
-        src_ref=asked, dst_ref=asked_next, send_sem=next_sem.at[0], recv_sem=next_sem.at[1],
+        src_ref=asked_2.at[1], dst_ref=asked_next, send_sem=next_sem.at[0], recv_sem=next_sem.at[1],
         device_id=(next_g, s), device_id_type=MESH,
     )
 
@@ -176,7 +184,7 @@
         first = 0 if t else 1
         negs, got, back = negs_2.at[t], got_2.at[t], back_2.at[t]
         pair_got, neg_got, rel_rows = pair_got_2.at[t], neg_got_2.at[t], rel_rows_2.at[t]
-        wanted = asked_next if t else asked
+        wanted = asked_next if t else asked_2.at[0]
         limit = lengths[t, 0, 0]
 
         def live(i):
@@ -219,25 +227,25 @@
                 device_id=(from_g, along(k)), device_id_type=MESH,
             )
 
-        def grad_copy(k):
+        def query_copy(k):
             target = lax.rem(s + k, shards)
             return pltpu.make_async_remote_copy(
-                src_ref=chunk(sent, target, capacity), dst_ref=chunk(back, s, capacity),
+                src_ref=chunk(queries, target, capacity), dst_ref=chunk(back, s, capacity),
                 send_sem=grad_send.at[t, k], recv_sem=grad_recv.at[t, k],
                 device_id=(from_g, target), device_id_type=MESH,
             )
 
+        if t:
+            forward.wait()
+            name_negatives(asked_next)
+        else:
+            negs[pl.ds(pl.multiple_of(my_block * n_own, 16), n_own), :] = own_negs[...]
+        each(first, depth, lambda k: neg_copy(k).start())
+
         if t == 0:
-            each(1, shards, lambda k: request_copy(k).start())
-            asked[s] = requests[s]
-            asked[shards] = requests[shards]
-            negs[pl.ds(pl.multiple_of(my_block * n_own, 16), n_own), :] = own_negs[...]
-        else:
-            forward.wait()
-            name_negatives(1)
-        each(first, depth, lambda k: neg_copy(k).start())
-
-        if t == 0:
+            index_edges()
+            ask(0)
+            acc_t[...] = jnp.transpose(row_acc[...])
             for i in range(rel_steps):
                 load(i).wait()
                 value = chunks[i % 2]
@@ -247,13 +255,12 @@
                 low[at, :] = (value - top.astype(F32)).astype(BF16)
                 if i + 2 < rel_steps:
                     load(i + 2).start()
-            each(1, shards, lambda k: request_copy(k).wait())
-            forward.start()
+            each(1, shards, lambda k: request_copy(0, k).wait())
 
         def answer(who):
             columns = jnp.transpose(wanted[who])[:capacity, :]
             asked_t[pl.ds(pl.multiple_of(who * capacity, 16), capacity), :] = columns
-            return dot(hot(columns[:, t : t + 1], rows), table_bf[...]).astype(BF16)
+            return dot(hot(columns[:, 0:1], rows), table_bf[...]).astype(BF16)
 
         def send_rows(k):
             target = lax.rem(s + k, shards)
@@ -262,7 +269,9 @@
 
         each(first, shards, send_rows)
         if t == 0:
-            got[pl.ds(pl.multiple_of(s * capacity, 16), capacity), :] = answer(s)
+            own_block = pl.ds(pl.multiple_of(s * capacity, 16), capacity)
+            sent[own_block, :] = answer(s)
+            got[own_block, :] = sent[own_block, :]
         each(first, depth, lambda k: neg_copy(k).wait())
         neg_pair.start()
 
@@ -273,7 +282,7 @@
             at = pl.ds(pl.multiple_of(i * tile, 128), tile)
             emb = dot(hot(meta_t[at, :][:, 2 + t : 3 + t], rows), table_bf[...])
             src_emb[at, :] = emb.astype(BF16)
-            query_bf[at, :] = (emb * rel_rows[at, :]).astype(BF16)
+            query_bf[at, :] = jnp.where(live(i), emb * rel_rows[at, :], 0.0).astype(BF16)
             return carry
 
         lax.fori_loop(0, 3, look_sources, 0)
@@ -304,6 +313,27 @@
 
         each(0, edges // 128, mark_slots)
 
+        def mark_slots_t(i):
+            at = pl.multiple_of(i * 128, 128)
+            by_slot_t[pl.ds(at, 128), :] = hot_t(slot_row, 128, at)
+
+        slot_row = jnp.transpose(meta_t[...])[6 + t : 7 + t, :]
+        each(0, slots // 128, mark_slots_t)
+
+        def query_block(target):
+            at = pl.ds(pl.multiple_of(target * capacity, 16), capacity)
+            return dot(by_slot_t[at, :], query_bf[...]).astype(BF16)
+
+        def send_query(k):
+            target = lax.rem(s + k, shards)
+            queries[pl.ds(pl.multiple_of(target * capacity, 16), capacity), :] = query_block(target)
+            row_copy(k).wait_send()
+            query_copy(k).start()
+
+        each(first, shards, send_query)
+        if t == 0:
+            back[own_block, :] = query_block(s)
+
         pair_copy.wait()
         mine_side = pl.ds(pl.multiple_of(y_lo * n_side, 16), n_side)
         pair_sum[...] = (neg_send[mine_side, :].astype(F32) + pair_got[...].astype(F32)).astype(BF16)
@@ -311,19 +341,15 @@
             own = pl.ds(pl.multiple_of(z * n_own, 16), n_own)
             neg_got[own, :] = pair_sum[own, :]
         each(first, depth, lambda k: neg_grad_copy(k).start())
-
-        def mark_slots_t(i):
-            at = pl.multiple_of(i * 128, 128)
-            by_slot_t[pl.ds(at, 128), :] = hot_t(meta[6 + t : 7 + t, :], 128, at)
-
-        each(0, slots // 128, mark_slots_t)
-        asked_rows = jnp.transpose(asked_t[...])[t : t + 1, :]
+        asked_rows = jnp.transpose(asked_t[...])[0:1, :]
 
         def mark_asked(i):
             at = pl.multiple_of(i * 128, 128)
             by_asked_t[pl.ds(at, 128), :] = hot_t(asked_rows, 128, at)
 
         each(0, rows // 128, mark_asked)
+        if t == 0:
+            ask(1)
 
         n_half, n_quarter = n_rel // 2, n_rel // 4
         mine, theirs = core * n_half, (1 - core) * n_half
@@ -348,26 +374,9 @@
             grad = weight * dst + query_grad[at, :]
             src_grad[at, :] = (grad * rel).astype(BF16)
             rel_grad[at, :] = (grad * emb).astype(BF16)
-            dst_grad[at, :] = (weight * query).astype(BF16)
             return carry
 
         lax.fori_loop(0, 3, positives, 0)
-
-        def send_grads():
-            each(first, shards, lambda k: row_copy(k).wait_send())
-
-            def block(target):
-                at = pl.ds(pl.multiple_of(target * capacity, 16), capacity)
-                return dot(by_slot_t[at, :], dst_grad[...]).astype(BF16)
-
-            def send(k):
-                target = lax.rem(s + k, shards)
-                sent[pl.ds(pl.multiple_of(target * capacity, 16), capacity), :] = block(target)
-                grad_copy(k).start()
-
-            each(first, shards, send)
-            if t == 0:
-                back[pl.ds(pl.multiple_of(s * capacity, 16), capacity), :] = block(s)
 
         def scatter_sources():
             def step(i):
@@ -383,9 +392,23 @@
                 summed += neg_got[k * n_own : (k + 1) * n_own, :].astype(F32)
             upper = summed.astype(BF16)
             lower = (summed - upper.astype(F32)).astype(BF16)
-            picked = hot_t(wanted[shards][t : t + 1, :n_own], rows)
+            picked = hot_t(wanted[shards][0:1, :n_own], rows)
             total[...] += dot(picked, upper) + dot(picked, lower)
-            each(first, shards, lambda k: grad_copy(k).wait())
+
+            def weigh(who):
+                at = pl.ds(pl.multiple_of(who * capacity, 16), capacity)
+                query = back[at, :].astype(F32)
+                positive = jnp.sum(query * sent[at, :].astype(F32), axis=1, keepdims=True)
+                weight = (jnp.tanh(positive * -0.5) + 1.0) * -0.5
+                back[at, :] = (weight * query).astype(BF16)
+
+            def take_one(k):
+                query_copy(k).wait()
+                weigh(lax.rem(s + shards - k, shards))
+
+            if t == 0:
+                weigh(s)
+            each(first, shards, take_one)
             for i in range(rows // 128):
                 at = slice(i * 128, i * 128 + 128)
                 grad = total[at, :] + dot(by_asked_t[at, :], back[...])
@@ -397,7 +420,6 @@
                     table_bf[at, :] = fresh.astype(BF16)
 
         if t == 0:
-            send_grads()
             scatter_sources()
 
             def scatter(i):
@@ -407,6 +429,8 @@
 
             each(0, n_rel // 512, scatter)
             look_relations(1)
+            each(1, shards, lambda k: request_copy(1, k).wait())
+            forward.start()
             take_grads()
             return
 
@@ -440,7 +464,6 @@
 
         each(0, n_half // 512, scatter_theirs)
         copies = run([rel_copy(span(half, theirs, n_half), rel_got_c, 0, core_dev)])
-        send_grads()
         each(0, n_half // 512, scatter_mine)
         finish(copies)
 
@@ -498,10 +521,9 @@
             [rel_copy(*same(mine + x * big, big), 32 + k, x_dev(k)) for k in (1, 2, 3)]
             + [rel_copy(*same(mine + n_quarter + y * big, big), 35 + k, y_dev(k)) for k in (1, 2, 3)]
         )
-        finish(copies)
-        copies = run([rel_copy(*same(mine, n_half), 39, core_dev)])
         take_grads()
         finish(copies)
+        finish(run([rel_copy(*same(mine, n_half), 39, core_dev)]))
 
     round_of(0)
     round_of(1)
@@ -520,18 +542,18 @@
     sems = lambda *shape: pltpu.SemaphoreType.DMA(shape)
     scratch = [
         i32(8, edges), i32(edges, 8),
-        i32(shards + 1, 8, LANES), i32(shards + 1, 8, LANES), i32(shards + 1, 8, LANES), i32(slots, 8),
+        i32(2, shards + 1, 8, LANES), i32(2, shards + 1, 8, LANES), i32(shards + 1, 8, LANES), i32(slots, 8),
         f32(2, 512), bf(n_rel), bf(n_rel), bf(rows), pltpu.VMEM((rows // 8, 8), F32),
-        bf(n_own), bf(2, n_neg), bf(slots), bf(2, slots), bf(2, slots),
+        bf(n_own), bf(2, n_neg), bf(slots), bf(slots), bf(2, slots), bf(2, slots),
         bf(n_neg), bf(2, n_neg // 2), bf(n_neg // 2), bf(2, n_neg // 2),
-        bf(edges), f32(2, edges), bf(edges), f32(edges), bf(edges), bf(edges), bf(edges),
+        bf(edges), f32(2, edges), bf(edges), f32(edges), bf(edges), bf(edges),
         pltpu.VMEM((width, n_neg), F32), f32(rows),
         pltpu.VMEM((edges, slots), BF16), pltpu.VMEM((slots, edges), BF16),
         pltpu.VMEM((rows, slots), BF16), pltpu.VMEM((n_rel // 2, edges), BF16),
         bf(n_rel), bf(n_rel // 2),
         bf(3, n_rel // 16), bf(3, n_rel // 16), bf(n_rel // 16), bf(n_rel // 16),
         bf(3, n_rel // 64), bf(3, n_rel // 64), bf(n_rel // 32), bf(7, n_rel // 256),
-        sems(2), sems(shards), sems(shards), sems(2, 2, depth + 1),
+        sems(2), sems(2, shards), sems(2, shards), sems(2, 2, depth + 1),
         sems(2, shards), sems(2, shards), sems(2, 2),
         sems(2, depth), sems(2, depth), sems(2, shards), sems(2, shards),
         sems(2), sems(40), sems(40),

time: 202 us -> 200 us (0.990)
    pallas_call x1, Pallas kernels: 190 us -> 188 us  [train(): pl.pallas_call(functools.partial(train_kernel, groups, shards, edges, cap...]
where the time goes in v3:
time: 200 us; the launch traced here: 199 us
  Pallas kernels  188 us (94%)
  other arithmetic  7.39 us (4%)
  local copies, waits for them, and re-layouts  2.88 us (1%)
    pallas_call x1, Pallas kernels, train(): pl.pallas_call(functools.partial(train_kernel, groups, shards, edges, cap...  188 us
    sub x1, other arithmetic, adagrad(): return (table - LEARN_RATE * gradient / jnp.sqrt(total)[..., None], total)  4.57 us

profile of v3, /device:TPU:1, one launch (start us, length us, event | category | flops | bytes accessed | tf_op | source)
XLA Modules:
  0.0 199.3 jit_solution(12159638105686716288)
XLA Ops:
  0.6 0.0 copy-start.1
  0.6 1.3 copy.14.refs_8_
  1.9 188.4 %train.1 = (f32[1024,256]{1,0:T(8,128)}, f32[8,128]{1,0:T(8,128)}, bf16[4096,256]{1,0:T(8,128)(2,1)}) custom-call(f32[1024,256]{1,0:T(8,128)} %refs_0_.1, f32[8,128]{1,0:T(8,128)} %bitcast.4, f32[4096,256]{1,0:T(8,128)} %refs_2_.1, s32[2,1,1,1152]{3,2,1,0:T(1,128)} %refs_3_.1, s32[2,1,1,1152]{3,2,1,0:T(1,128)} %refs_4_.1, s32[2,1,1,1152]{3,2,1,0:T(1,128)} %bitcast.3, ...), custom_call_target="tpu_custom_call" | custom-call | tf_op jit(solution)/shard_map/train/pallas_call | solution.py:562
  190.3 2.2 %fusion.2 = f32[4096]{0:T(1024)S(1)} fusion(bf16[4096,256]{1,0:T(8,128)(2,1)} %get-tuple-element.9), kind=kLoop, calls=%fused_computation.4 | loop fusion | flops 3141632 | bytes 2113536 | tf_op jit(solution)/shard_map/reduce_sum | solution.py:17
  192.5 0.0 copy-done.1
  192.5 0.6 fusion.3
  193.1 0.0 copy-start
  193.1 0.0 copy-start.2
  193.1 4.6 %fusion.1 = f32[4096,256]{1,0:T(8,128)} fusion(f32[4096,256]{1,0:T(8,128)} %refs_2_.1, bf16[4096,256]{1,0:T(8,128)(2,1)} %get-tuple-element.9, f32[4096]{0:T(1024)S(1)} %get-tuple-element.10), kind=kLoop, calls=%fused_computation.3 | loop fusion | flops 4194304 | bytes 10502144 | tf_op jit(solution)/shard_map/sub | solution.py:18
  197.7 0.0 copy-done
  197.7 1.0 copy.17
  198.7 0.0 copy-done.2
  198.7 0.6 copy.18
Async XLA Ops:
  0.6 191.9 %copy-start.1 = (f32[4096]{0:T(1024)S(1)}, f32[4096]{0:T(1024)}, u32[]{:S(2)}) copy-start(f32[4096]{0:T(1024)} %param.13) | copy-start | bytes 49156
  193.1 4.6 %copy-start = (f32[1024,256]{1,0:T(8,128)S(1)}, f32[1024,256]{1,0:T(8,128)}, u32[]{:S(2)}) copy-start(f32[1024,256]{1,0:T(8,128)} %get-tuple-element.16) | copy-start | bytes 3145732
  193.1 5.5 %copy-start.2 = (f32[8,128]{1,0:T(8,128)S(1)}, f32[8,128]{1,0:T(8,128)}, u32[]{:S(2)}) copy-start(f32[8,128]{1,0:T(8,128)} %get-tuple-element.8) | copy-start | bytes 12292

commit v4 on v3

--- a/solution.py
+++ b/solution.py
@@ -110,8 +110,6 @@
         own_negs[...] = dot(hot(column, rows), table_bf[...]).astype(BF16)
 
     name_negatives(requests_2.at[0])
-    pl.semaphore_wait(barrier, shards - 1 + len(others))
-
     def index_edges():
         for t in range(2):
             meta[t : t + 1, :] = dst_owner[t, 0]
@@ -159,10 +157,13 @@
         )
 
     def ask(t):
-        plan(t)
         each(1, shards, lambda k: request_copy(t, k).start())
         asked_2[t, s] = requests_2[t, s]
         asked_2[t, shards] = requests_2[t, shards]
+
+    index_edges()
+    plan(0)
+    pl.semaphore_wait(barrier, shards - 1 + len(others))
 
     forward = pltpu.make_async_remote_copy(
         src_ref=asked_2.at[1], dst_ref=asked_next, send_sem=next_sem.at[0], recv_sem=next_sem.at[1],
@@ -185,7 +186,7 @@
         negs, got, back = negs_2.at[t], got_2.at[t], back_2.at[t]
         pair_got, neg_got, rel_rows = pair_got_2.at[t], neg_got_2.at[t], rel_rows_2.at[t]
         wanted = asked_next if t else asked_2.at[0]
-        limit = lengths[t, 0, 0]
+        limit = lengths[0:1, t : t + 1]
 
         def live(i):
             place = lax.broadcasted_iota(jnp.int32, (tile, 1), 0) + i * tile
@@ -239,12 +240,11 @@
             forward.wait()
             name_negatives(asked_next)
         else:
+            ask(0)
             negs[pl.ds(pl.multiple_of(my_block * n_own, 16), n_own), :] = own_negs[...]
         each(first, depth, lambda k: neg_copy(k).start())
 
         if t == 0:
-            index_edges()
-            ask(0)
             acc_t[...] = jnp.transpose(row_acc[...])
             for i in range(rel_steps):
                 load(i).wait()
@@ -320,6 +320,24 @@
         slot_row = jnp.transpose(meta_t[...])[6 + t : 7 + t, :]
         each(0, slots // 128, mark_slots_t)
 
+        asked_rows = jnp.transpose(asked_t[...])[0:1, :]
+
+        def mark_asked(i):
+            at = pl.multiple_of(i * 128, 128)
+            by_asked_t[pl.ds(at, 128), :] = hot_t(asked_rows, 128, at)
+
+        each(0, rows // 128, mark_asked)
+
+        n_half, n_quarter = n_rel // 2, n_rel // 4
+        mine, theirs = core * n_half, (1 - core) * n_half
+        if t:
+
+            def mark_relations(i):
+                at = pl.multiple_of(i * 128, 128)
+                by_rel_t[pl.ds(at, 128), :] = hot_t(meta[4 + t : 5 + t, :], 128, theirs + at)
+
+            each(0, n_half // 128, mark_relations)
+
         def query_block(target):
             at = pl.ds(pl.multiple_of(target * capacity, 16), capacity)
             return dot(by_slot_t[at, :], query_bf[...]).astype(BF16)
@@ -340,28 +358,16 @@
         if t == 0:
             own = pl.ds(pl.multiple_of(z * n_own, 16), n_own)
             neg_got[own, :] = pair_sum[own, :]
-        each(first, depth, lambda k: neg_grad_copy(k).start())
-        asked_rows = jnp.transpose(asked_t[...])[0:1, :]
-
-        def mark_asked(i):
-            at = pl.multiple_of(i * 128, 128)
-            by_asked_t[pl.ds(at, 128), :] = hot_t(asked_rows, 128, at)
-
-        each(0, rows // 128, mark_asked)
-        if t == 0:
+        if t == 0:
+            each(1, depth, lambda k: neg_grad_copy(k).start())
+        if t == 0:
+            plan(1)
             ask(1)
 
-        n_half, n_quarter = n_rel // 2, n_rel // 4
-        mine, theirs = core * n_half, (1 - core) * n_half
-        if t:
-
-            def mark_relations(i):
-                at = pl.multiple_of(i * 128, 128)
-                by_rel_t[pl.ds(at, 128), :] = hot_t(meta[4 + t : 5 + t, :], 128, theirs + at)
-
-            each(0, n_half // 128, mark_relations)
-
         each(first, shards, lambda k: row_copy(k).wait_recv())
+
+        def send_held():
+            each(0, depth, lambda k: neg_grad_copy(k).start())
 
         def positives(i, carry):
             at = pl.ds(pl.multiple_of(i * tile, 128), tile)
@@ -385,33 +391,36 @@
 
             each(0, rows // 256, step)
 
-        def take_grads():
+        def take_queries():
+            each(first, shards, lambda k: query_copy(k).wait())
+
+            def weigh(i):
+                at = pl.ds(pl.multiple_of(i * 384, 128), 384)
+                query = back[at, :].astype(F32)
+                positive = jnp.sum(query * sent[at, :].astype(F32), axis=1, keepdims=True)
+                weight = (jnp.tanh(positive * -0.5) + 1.0) * -0.5
+                back[at, :] = (weight * query).astype(BF16)
+
+            each(0, slots // 384, weigh)
+
+            def add(i):
+                at = pl.ds(pl.multiple_of(i * 256, 256), 256)
+                total[at, :] += dot(by_asked_t[at, :], back[...])
+
+            each(0, rows // 256, add)
+
+        def take_negatives():
             each(first, depth, lambda k: neg_grad_copy(k).wait())
             summed = neg_got[0:n_own, :].astype(F32)
             for k in range(1, depth):
                 summed += neg_got[k * n_own : (k + 1) * n_own, :].astype(F32)
             upper = summed.astype(BF16)
             lower = (summed - upper.astype(F32)).astype(BF16)
-            picked = hot_t(wanted[shards][0:1, :n_own], rows)
-            total[...] += dot(picked, upper) + dot(picked, lower)
-
-            def weigh(who):
-                at = pl.ds(pl.multiple_of(who * capacity, 16), capacity)
-                query = back[at, :].astype(F32)
-                positive = jnp.sum(query * sent[at, :].astype(F32), axis=1, keepdims=True)
-                weight = (jnp.tanh(positive * -0.5) + 1.0) * -0.5
-                back[at, :] = (weight * query).astype(BF16)
-
-            def take_one(k):
-                query_copy(k).wait()
-                weigh(lax.rem(s + shards - k, shards))
-
-            if t == 0:
-                weigh(s)
-            each(first, shards, take_one)
+            named = wanted[shards][0:1, :n_own]
             for i in range(rows // 128):
                 at = slice(i * 128, i * 128 + 128)
-                grad = total[at, :] + dot(by_asked_t[at, :], back[...])
+                picked = hot_t(named, 128, i * 128)
+                grad = total[at, :] + dot(picked, upper) + dot(picked, lower)
                 acc = acc_t[:, i : i + 1] + jnp.sum(grad * grad, axis=1, keepdims=True) * (1.0 / width)
                 fresh = table[at, :] - LEARN_RATE * grad / jnp.sqrt(acc)
                 acc_t[:, i : i + 1] = acc
@@ -431,7 +440,8 @@
             look_relations(1)
             each(1, shards, lambda k: request_copy(1, k).wait())
             forward.start()
-            take_grads()
+            take_queries()
+            take_negatives()
             return
 
         big, small, least = n_quarter // 4, n_quarter // 16, n_rel // 256
@@ -462,8 +472,17 @@
             part = dot(hot_t(meta[5:6, :], 512, at), rel_grad[...])
             half[pl.ds(at, 512), :] = (half[pl.ds(at, 512), :].astype(F32) + part).astype(BF16)
 
-        each(0, n_half // 512, scatter_theirs)
-        copies = run([rel_copy(span(half, theirs, n_half), rel_got_c, 0, core_dev)])
+        copies = []
+        for i in range(2):
+            each(i * (n_half // 1024), (i + 1) * (n_half // 1024), scatter_theirs)
+            copies += run(
+                [
+                    rel_copy(
+                        span(half, theirs + i * n_quarter, n_quarter),
+                        span(rel_got_c, i * n_quarter, n_quarter), 40 * i, core_dev,
+                    )
+                ]
+            )
         each(0, n_half // 512, scatter_mine)
         finish(copies)
 
@@ -511,19 +530,21 @@
         rel_out[pl.ds(pl.multiple_of(at_z, 16), least), :] = sum_of(last, z * least, least, got_z)
         same = lambda at, size: [span(rel_out, at, size)] * 2
         finish(run([rel_copy(*same(at_z, least), 19 + k, z_dev(k)) for k in range(1, 8)]))
-        finish(
-            run(
-                [rel_copy(*same(at_x, small), 26 + k, y_dev(k)) for k in (1, 2, 3)]
-                + [rel_copy(*same(at_y, small), 29 + k, x_dev(k)) for k in (1, 2, 3)]
-            )
-        )
+        copies = run(
+            [rel_copy(*same(at_x, small), 26 + k, y_dev(k)) for k in (1, 2, 3)]
+            + [rel_copy(*same(at_y, small), 29 + k, x_dev(k)) for k in (1, 2, 3)]
+        )
+        send_held()
+        finish(copies)
         copies = run(
             [rel_copy(*same(mine + x * big, big), 32 + k, x_dev(k)) for k in (1, 2, 3)]
             + [rel_copy(*same(mine + n_quarter + y * big, big), 35 + k, y_dev(k)) for k in (1, 2, 3)]
         )
-        take_grads()
+        take_queries()
         finish(copies)
-        finish(run([rel_copy(*same(mine, n_half), 39, core_dev)]))
+        copies = run([rel_copy(*same(mine, n_half), 39, core_dev)])
+        take_negatives()
+        finish(copies)
 
     round_of(0)
     round_of(1)
@@ -556,7 +577,7 @@
         sems(2), sems(2, shards), sems(2, shards), sems(2, 2, depth + 1),
         sems(2, shards), sems(2, shards), sems(2, 2),
         sems(2, depth), sems(2, depth), sems(2, shards), sems(2, shards),
-        sems(2), sems(40), sems(40),
+        sems(2), sems(41), sems(41),
     ]
     vmem = pl.BlockSpec(memory_space=pltpu.VMEM)
     return pl.pallas_call(
@@ -566,17 +587,16 @@
             jax.ShapeDtypeStruct((8, rows // 8), F32),
             jax.ShapeDtypeStruct((n_rel, width), BF16),
         ],
-        in_specs=[vmem, vmem, pl.BlockSpec(memory_space=pl.ANY)] + [vmem] * 5
-        + [pl.BlockSpec(memory_space=pltpu.SMEM)],
+        in_specs=[vmem, vmem, pl.BlockSpec(memory_space=pl.ANY)] + [vmem] * 6,
         out_specs=[vmem] * 3,
         scratch_shapes=scratch,
         compiler_params=pltpu.CompilerParams(
-            collective_id=0, has_side_effects=True, vmem_limit_bytes=60 << 20
+            collective_id=0, has_side_effects=True, vmem_limit_bytes=56 << 20
         ),
         name="train",
     )(
         entities, row_acc.reshape(8, rows // 8), relations, src_row, rel_id,
-        dst_owner[..., 0], dst_row, neg_rows, lengths,
+        dst_owner[..., 0], dst_row, neg_rows, lengths.reshape(1, 2),
     )
 
 

time: 200 us -> 193 us (0.965)
  Pallas kernels: 188 us -> 184 us
    pallas_call x1, Pallas kernels: 188 us -> 184 us  [train(): pl.pallas_call(functools.partial(train_kernel, groups, shards, edges, cap...]
where the time goes in v4:
time: 193 us
  Pallas kernels  184 us (95%)
  other arithmetic  6.51 us (3%)
    pallas_call x1, Pallas kernels, train(): pl.pallas_call(functools.partial(train_kernel, groups, shards, edges, cap...  184 us

profile of v4, /device:TPU:1, one launch (start us, length us, event | category | flops | bytes accessed | tf_op | source)
XLA Modules:
  0.0 193.0 jit_solution(13364887819996134045)
XLA Ops:
  0.6 0.0 copy-start
  0.6 0.0 copy-start.2
  0.7 184.3 %train.1 = (f32[1024,256]{1,0:T(8,128)}, f32[8,128]{1,0:T(8,128)}, bf16[4096,256]{1,0:T(8,128)(2,1)}) custom-call(f32[1024,256]{1,0:T(8,128)} %refs_0_.1, f32[8,128]{1,0:T(8,128)} %bitcast.5, f32[4096,256]{1,0:T(8,128)} %refs_2_.1, s32[2,1,1,1152]{3,2,1,0:T(1,128)} %refs_3_.1, s32[2,1,1,1152]{3,2,1,0:T(1,128)} %refs_4_.1, s32[2,1,1,1152]{3,2,1,0:T(1,128)} %bitcast.4, ...), custom_call_target="tpu_custom_call" | custom-call | tf_op jit(solution)/shard_map/train/pallas_call | solution.py:583
  184.9 2.2 %fusion.2 = f32[4096]{0:T(1024)S(1)} fusion(bf16[4096,256]{1,0:T(8,128)(2,1)} %get-tuple-element.9), kind=kLoop, calls=%fused_computation.4 | loop fusion | flops 3141632 | bytes 2113536 | tf_op jit(solution)/shard_map/reduce_sum | solution.py:17
  187.2 0.0 copy-done.2
  187.2 0.6 fusion.3
  187.8 0.0 copy-done
  187.8 0.0 copy-start.1
  187.8 0.0 copy-start.3
  187.8 3.7 %fusion.1 = f32[4096,256]{1,0:T(8,128)} fusion(f32[4096,256]{1,0:T(8,128)S(1)} %copy-done, bf16[4096,256]{1,0:T(8,128)(2,1)} %get-tuple-element.9, f32[4096]{0:T(1024)S(1)} %get-tuple-element.10), kind=kLoop, calls=%fused_computation.3 | loop fusion | flops 4194304 | bytes 10502144 | tf_op jit(solution)/shard_map/sub | solution.py:18
  191.5 0.0 copy-done.1
  191.5 1.0 copy.16
  192.4 0.0 copy-done.3
  192.4 0.6 copy.17
Async XLA Ops:
  0.6 187.1 %copy-start = (f32[4096,256]{1,0:T(8,128)S(1)}, f32[4096,256]{1,0:T(8,128)}, u32[]{:S(2)}) copy-start(f32[4096,256]{1,0:T(8,128)} %refs_2_.1) | copy-start | bytes 12582916
  0.6 186.5 %copy-start.2 = (f32[4096]{0:T(1024)S(1)}, f32[4096]{0:T(1024)}, u32[]{:S(2)}) copy-start(f32[4096]{0:T(1024)} %param.13) | copy-start | bytes 49156
  187.8 3.7 %copy-start.1 = (f32[1024,256]{1,0:T(8,128)S(1)}, f32[1024,256]{1,0:T(8,128)}, u32[]{:S(2)}) copy-start(f32[1024,256]{1,0:T(8,128)} %get-tuple-element.16) | copy-start | bytes 3145732
  187.8 4.7 %copy-start.3 = (f32[8,128]{1,0:T(8,128)S(1)}, f32[8,128]{1,0:T(8,128)}, u32[]{:S(2)}) copy-start(f32[8,128]{1,0:T(8,128)} %get-tuple-element.8) | copy-start | bytes 12292

commit v5 on v4

--- a/solution.py
+++ b/solution.py
@@ -13,11 +13,6 @@
 LANES = 256
 
 
-def adagrad(table, accum, gradient):
-    total = accum + jnp.mean(gradient * gradient, axis=-1)
-    return (table - LEARN_RATE * gradient / jnp.sqrt(total)[..., None], total)
-
-
 def dot(a, b):
     return jnp.dot(a, b, preferred_element_type=F32)
 
@@ -34,8 +29,8 @@
 
 def train_kernel(groups, shards, edges, capacity, n_own, *refs):
     (entities, row_acc, relations, src_row, rel_id, dst_owner, dst_row, neg_rows, lengths,
-     table, acc_out, rel_out,
-     meta, meta_t, requests_2, asked_2, asked_next, asked_t, chunks, high, low, table_bf, acc_t,
+     table, acc_out, rel_out, square_out,
+     meta, meta_t, requests_2, asked_2, asked_next, asked_t, chunks, high, low, table_bf, acc_t, square_t,
      own_negs, negs_2, sent, queries, got_2, back_2, neg_send, pair_got_2, pair_sum, neg_got_2,
      src_emb, rel_rows_2, query_bf, query_grad, src_grad, rel_grad, neg_acc, total,
      by_slot, by_slot_t, by_asked_t, by_rel_t,
@@ -287,6 +282,31 @@
 
         lax.fori_loop(0, 3, look_sources, 0)
 
+        slot_row = jnp.transpose(meta_t[...])[6 + t : 7 + t, :]
+
+        def mark_slots_t(i):
+            at = pl.multiple_of(i * 128, 128)
+            by_slot_t[pl.ds(at, 128), :] = hot_t(slot_row, 128, at)
+
+        def query_block(target):
+            at = pl.ds(pl.multiple_of(target * capacity, 16), capacity)
+            return dot(by_slot_t[at, :], query_bf[...]).astype(BF16)
+
+        def send_query(k):
+            target = lax.rem(s + k, shards)
+            queries[pl.ds(pl.multiple_of(target * capacity, 16), capacity), :] = query_block(target)
+            if t:
+                row_copy(k).wait_send()
+            query_copy(k).start()
+
+        def send_queries():
+            each(0, slots // 128, mark_slots_t)
+            each(first, shards, send_query)
+            if t == 0:
+                back[own_block, :] = query_block(s)
+
+        if t == 0:
+            send_queries()
         neg_pair.wait()
         neg_acc[...] = jnp.zeros_like(neg_acc)
 
@@ -313,13 +333,6 @@
 
         each(0, edges // 128, mark_slots)
 
-        def mark_slots_t(i):
-            at = pl.multiple_of(i * 128, 128)
-            by_slot_t[pl.ds(at, 128), :] = hot_t(slot_row, 128, at)
-
-        slot_row = jnp.transpose(meta_t[...])[6 + t : 7 + t, :]
-        each(0, slots // 128, mark_slots_t)
-
         asked_rows = jnp.transpose(asked_t[...])[0:1, :]
 
         def mark_asked(i):
@@ -338,20 +351,8 @@
 
             each(0, n_half // 128, mark_relations)
 
-        def query_block(target):
-            at = pl.ds(pl.multiple_of(target * capacity, 16), capacity)
-            return dot(by_slot_t[at, :], query_bf[...]).astype(BF16)
-
-        def send_query(k):
-            target = lax.rem(s + k, shards)
-            queries[pl.ds(pl.multiple_of(target * capacity, 16), capacity), :] = query_block(target)
-            row_copy(k).wait_send()
-            query_copy(k).start()
-
-        each(first, shards, send_query)
-        if t == 0:
-            back[own_block, :] = query_block(s)
-
+        if t:
+            send_queries()
         pair_copy.wait()
         mine_side = pl.ds(pl.multiple_of(y_lo * n_side, 16), n_side)
         pair_sum[...] = (neg_send[mine_side, :].astype(F32) + pair_got[...].astype(F32)).astype(BF16)
@@ -364,6 +365,8 @@
             plan(1)
             ask(1)
 
+        if t == 0:
+            each(1, shards, lambda k: row_copy(k).wait_send())
         each(first, shards, lambda k: row_copy(k).wait_recv())
 
         def send_held():
@@ -544,7 +547,24 @@
         finish(copies)
         copies = run([rel_copy(*same(mine, n_half), 39, core_dev)])
         take_negatives()
+
+        def square(begin):
+            for i in range(n_half // 128):
+                at = pl.ds(pl.multiple_of(begin + i * 128, 128), 128)
+                value = rel_out[at, :].astype(F32)
+                square_t[:, part_of + i : part_of + i + 1] = jnp.sum(
+                    value * value, axis=1, keepdims=True
+                )
+
+        part_of = 0
+        square(mine)
         finish(copies)
+        part_of = n_half // 128
+        square(theirs)
+        squares = jnp.transpose(square_t[...])
+        part_of = n_half // 128
+        square_out[pl.ds(pl.multiple_of(core * part_of, 8), part_of), :] = squares[:part_of, :]
+        square_out[pl.ds(pl.multiple_of((1 - core) * part_of, 8), part_of), :] = squares[part_of:, :]
 
     round_of(0)
     round_of(1)
@@ -565,6 +585,7 @@
         i32(8, edges), i32(edges, 8),
         i32(2, shards + 1, 8, LANES), i32(2, shards + 1, 8, LANES), i32(shards + 1, 8, LANES), i32(slots, 8),
         f32(2, 512), bf(n_rel), bf(n_rel), bf(rows), pltpu.VMEM((rows // 8, 8), F32),
+        pltpu.VMEM((128, n_rel // 128), F32),
         bf(n_own), bf(2, n_neg), bf(slots), bf(slots), bf(2, slots), bf(2, slots),
         bf(n_neg), bf(2, n_neg // 2), bf(n_neg // 2), bf(2, n_neg // 2),
         bf(edges), f32(2, edges), bf(edges), f32(edges), bf(edges), bf(edges),
@@ -586,9 +607,10 @@
             jax.ShapeDtypeStruct((rows, width), F32),
             jax.ShapeDtypeStruct((8, rows // 8), F32),
             jax.ShapeDtypeStruct((n_rel, width), BF16),
+            jax.ShapeDtypeStruct((n_rel // 128, 128), F32),
         ],
         in_specs=[vmem, vmem, pl.BlockSpec(memory_space=pl.ANY)] + [vmem] * 6,
-        out_specs=[vmem] * 3,
+        out_specs=[vmem] * 4,
         scratch_shapes=scratch,
         compiler_params=pltpu.CompilerParams(
             collective_id=0, has_side_effects=True, vmem_limit_bytes=56 << 20
@@ -603,10 +625,11 @@
 def per_device(
     entities, row_acc, relations, rel_acc, src_row, rel_id, dst_owner, dst_row, neg_rows, lengths
 ):
-    table, accum, rel_total = train(
+    table, accum, rel_total, square = train(
         entities, row_acc, relations, src_row, rel_id, dst_owner, dst_row, neg_rows, lengths
     )
-    new_rel, new_racc = adagrad(relations, rel_acc, rel_total.astype(F32))
+    new_racc = rel_acc + square.reshape(-1) * (1.0 / relations.shape[1])
+    new_rel = relations - LEARN_RATE * rel_total.astype(F32) / jnp.sqrt(new_racc)[:, None]
     return (table, accum.reshape(-1), new_rel, new_racc)
 
 

time: 193 us -> 191 us (0.990)
    reduce_sum x1 -> x0, other arithmetic: 2.21 us -> none  [adagrad(): total = accum + jnp.mean(gradient * gradient, axis=-1)]
where the time goes in v5:
time: 191 us; the launch traced here: 190 us
  Pallas kernels  183 us (96%)
  other arithmetic  5.02 us (3%)
    pallas_call x1, Pallas kernels, train(): pl.pallas_call(functools.partial(train_kernel, groups, shards, edges, cap...  183 us

profile of v5, /device:TPU:1, one launch (start us, length us, event | category | flops | bytes accessed | tf_op | source)
XLA Modules:
  0.0 190.4 jit_solution(6519310185718648034)
XLA Ops:
  0.6 0.0 copy-start
  0.6 0.0 copy-start.2
  0.7 183.1 %train.1 = (f32[1024,256]{1,0:T(8,128)}, f32[8,128]{1,0:T(8,128)}, bf16[4096,256]{1,0:T(8,128)(2,1)}, f32[32,128]{1,0:T(8,128)}) custom-call(f32[1024,256]{1,0:T(8,128)} %refs_0_.1, f32[8,128]{1,0:T(8,128)} %bitcast.8, f32[4096,256]{1,0:T(8,128)} %refs_2_.1, s32[2,1,1,1152]{3,2,1,0:T(1,128)} %refs_3_.1, s32[2,1,1,1152]{3,2,1,0:T(1,128)} %refs_4_.1, ...), custom_call_target="tpu_custom_call" | custom-call | tf_op jit(solution)/shard_map/train/pallas_call | solution.py:604
  183.8 0.0 copy-done.2
  183.8 1.3 fusion
  185.1 0.0 copy-done
  185.1 0.0 copy-start.1
  185.1 0.0 copy-start.3
  185.1 3.7 %divide_subtract_fusion = f32[4096,256]{1,0:T(8,128)} fusion(f32[4096,256]{1,0:T(8,128)S(1)} %copy-done, bf16[4096,256]{1,0:T(8,128)(2,1)} %get-tuple-element.10, f32[4096]{0:T(1024)S(1)} %get-tuple-element.12), kind=kLoop, calls=%fused_computation | loop fusion | flops 4194304 | bytes 10502144 | tf_op jit(solution)/shard_map/sub | solution.py:632
  188.8 0.0 copy-done.1
  188.8 1.0 copy.16
  189.8 0.0 copy-done.3
  189.8 0.6 copy.17
Async XLA Ops:
  0.6 184.5 %copy-start = (f32[4096,256]{1,0:T(8,128)S(1)}, f32[4096,256]{1,0:T(8,128)}, u32[]{:S(2)}) copy-start(f32[4096,256]{1,0:T(8,128)} %refs_2_.1) | copy-start | bytes 12582916
  0.6 183.1 %copy-start.2 = (f32[4096]{0:T(1024)S(1)}, f32[4096]{0:T(1024)}, u32[]{:S(2)}) copy-start(f32[4096]{0:T(1024)} %param.13) | copy-start | bytes 49156
  185.1 3.7 %copy-start.1 = (f32[1024,256]{1,0:T(8,128)S(1)}, f32[1024,256]{1,0:T(8,128)}, u32[]{:S(2)}) copy-start(f32[1024,256]{1,0:T(8,128)} %get-tuple-element.18) | copy-start | bytes 3145732
  185.1 4.7 %copy-start.3 = (f32[8,128]{1,0:T(8,128)S(1)}, f32[8,128]{1,0:T(8,128)}, u32[]{:S(2)}) copy-start(f32[8,128]{1,0:T(8,128)} %get-tuple-element.9) | copy-start | bytes 12292
